TPU v7x, 512 devices: a whole 4x4x16 slice. The times are simulated.
512 devices in a mesh: front: 16 (over y, z_lo), blk: 32 (over z_hi, x, core).
Axes of the slice: x: 4, y: 4, z: 16 (z_hi: 4, z_lo: 4; z = z_hi * 4 + z_lo), core: 2. Of those that a mesh axis runs over, the one named last changes fastest.
Arguments:
- parent_inverse: bfloat16 [16, 4096, 8192], P('front', 'blk'), may hold values from -6 to 6
- child_factor: bfloat16 [16, 5120, 512], P('front', 'blk'), may hold values from -0.078125 to 0.078125
- child_diagonal: float32 [16, 512, 512], P('front', 'blk'), may hold values from -6 to 6
- structure: int32 [16, 40], replicated, may hold values from 0 to 63, as said below
Outputs:
- off_diagonal: float32 [16, 4096, 2, 512], P('front', 'blk')
- child_inverse: float32 [16, 512, 512], P('front', 'blk')
Inputs may be any that keep to these rules, and one draw needn't show every extreme that they name: `structure`: each row lists 40 distinct parent block indices in increasing order, and every list contains the last block 63.
All inputs are finite; a program needn't handle non-finite values.
Results may differ from a plain program's by a relative error of at most 0.002.
Values may be sent and summed in bfloat16 or wider, within the bound.
No kernel may reach another device: no remote copies, remote signals or barrier semaphores. Data moves between devices by JAX's collectives and lax.ppermute only.
A program may use at most 64 MiB of HBM per device.

v0:
```python
import jax
import jax.numpy as jnp
from jax import lax
from jax.sharding import PartitionSpec as P

BS = 128
NPB = 64
NS = 40
NC = 512


def partner(value, axis, apart):
    mask = 2**apart
    pairs = [(source, source ^ mask) for source in range(lax.axis_size(axis))]
    return lax.ppermute(value, axis, pairs)


def body(parent_inverse, child_factor, child_diagonal, structure):
    parent_rows = parent_inverse[0]
    local_count = parent_rows.shape[0] // BS
    blk_index = lax.axis_index("blk")
    front_index = lax.axis_index("front")
    half = front_index % 2
    partner_index = front_index - half + 1 - half
    own_list = lax.dynamic_index_in_dim(structure, front_index, 0, keepdims=False)
    other_list = lax.dynamic_index_in_dim(structure, partner_index, 0, keepdims=False)
    own_whole = lax.all_gather(child_factor, "blk", axis=1, tiled=True)
    other_whole = partner(own_whole, "front", 0)
    factors = (own_whole[0], other_whole[0])
    listings = (own_list, other_list)
    first_block = half * (NPB // 2) + blk_index * local_count
    products = []
    rounded = []
    factor_blocks = []
    for child_slot in range(2):
        listing = listings[child_slot]
        factor = factors[child_slot]
        slot_index = 0
        block_index = first_block + slot_index
        member = jnp.any(listing == block_index)
        position = jnp.minimum(jnp.sum((listing < block_index).astype(jnp.int32)), NS - 1)
        block_rows = parent_rows

        def compute(block_rows=block_rows, listing=listing, factor=factor):
            restricted = jnp.take(block_rows.reshape(BS, NPB, BS), listing, axis=1)
            restricted = restricted.reshape(BS, NS * BS)
            return jnp.dot(restricted, factor, preferred_element_type=jnp.float32)

        def nothing():
            return jnp.zeros((BS, NC), jnp.float32)

        block_product = lax.cond(member, compute, nothing)
        slot_products = [block_product]
        slot_rounded = [block_product.astype(jnp.bfloat16)]
        slot_blocks = [lax.dynamic_slice_in_dim(factor, position * BS, BS, 0)]
        products.append(slot_products)
        rounded.append(slot_rounded)
        factor_blocks.append(slot_blocks)
    placed = jnp.stack(
        [-jnp.concatenate(products[0], axis=0), -jnp.concatenate(products[1], axis=0)], axis=1
    )
    pieces = []
    for child_slot in range(2):
        slot_index = 0
        left_part = factor_blocks[child_slot][slot_index]
        accum = jnp.dot(
            left_part.T, rounded[child_slot][slot_index], preferred_element_type=jnp.float32
        )
        pieces.append(accum)
    summed = lax.psum_scatter(
        jnp.concatenate(pieces, axis=1), "blk", scatter_dimension=0, tiled=True
    )
    from_partner = partner(summed[:, NC:], "front", 0)
    inverse = child_diagonal[0] + summed[:, :NC] + from_partner
    return (placed[None], inverse[None])


def solution(mesh):
    in_specs = (P("front", "blk", None), P("front", "blk", None), P("front", "blk", None), P())
    out_specs = (P("front", "blk", None, None), P("front", "blk", None))
    return jax.shard_map(body, mesh=mesh, in_specs=in_specs, out_specs=out_specs, check_vma=False)
```

profile of v0, /device:TPU:1, one launch (start us, length us, event | category | flops | bytes accessed | tf_op | source)
XLA Modules:
  0.0 392.3 jit_solution(12689149762742840662)
XLA Ops:
  7.2 0.7 all-gather.2.cloned.1.call-update
  7.9 116.1 %all-gather.2.cloned.1.call-done = bf16[1,5120,512]{2,1,0:T(8,128)(2,1)} async-done(((bf16[1,160,512]{2,1,0:T(8,128)(2,1)}), bf16[1,5120,512]{2,1,0:T(8,128)(2,1)}) %all-gather.2.cloned.1.call-update) | async-done | bytes 5242896 | tf_op jit(solution)/shard_map/all_gather | solution.py:27
  124.1 1.9 collective-permute-start
  126.0 1.4 fusion.18
  128.7 0.6 compare_reduce_fusion
  130.0 0.6 compare_reduce_fusion.1
  131.3 13.0 %conditional.2 = (f32[128,512]{1,0:T(8,128)S(1)}) conditional(s32[]{:T(128)} %convert_element_type.18, () %tuple.21, (bf16[1,128,8192]{2,1,0:T(8,128)(2,1)}, s32[40]{0:T(128)S(1)}, bf16[1,5120,512]{2,1,0:T(8,128)(2,1)}) %tuple.22), branch_computations={%region_1.2_spmd, %region_2.4_spmd} | conditional | flops 671745408 | bytes 23073656 | solution.py:52
  131.4 3.2 copy.22
  134.6 2.9 copy.18
  137.5 2.4 gather_fusion
  139.9 0.2 select_bitcast_fusion
  140.1 0.8 copy.19
  140.9 3.4 fusion
  144.3 2.2 fusion.8
  146.5 94.2 %collective-permute-done = bf16[1,5120,512]{2,1,0:T(8,128)(2,1)} collective-permute-done((bf16[1,5120,512]{2,1,0:T(8,128)(2,1)}, bf16[1,5120,512]{2,1,0:T(8,128)(2,1)}, u32[]{:S(2)}, u32[]{:S(2)}) %collective-permute-start) | collective-permute-done | bytes 5242912 | tf_op jit(solution)/shard_map/ppermute | solution.py:15
  240.7 0.7 conditional.3
  240.7 0.7 broadcast.9
  241.4 1.4 fusion.6
  242.8 0.2 pad_maximum_fusion
  243.0 1.9 copy.26
  244.9 0.7 copy-done.1
  245.7 0.1 copy.24
  245.8 0.2 stack.9
  246.0 1.0 neg.7
  247.0 0.2 stack.10
  247.2 128.6 %reduce-scatter.4.cloned.1.call-done = f32[16,1024]{1,0:T(8,128)} async-done(((f32[512,1024]{1,0:T(8,128)}), f32[16,1024]{1,0:T(8,128)}) %reduce-scatter.4.cloned.1.call-update) | async-done | bytes 65552
  375.8 0.8 fusion.22
  376.6 0.1 copy.29
  376.7 1.9 collective-permute-start.1
  378.6 1.3 maximum_bitcast_fusion
  380.0 4.7 %collective-permute-done.1 = f32[16,512]{0,1:T(8,128)S(1)} collective-permute-done((f32[16,512]{0,1:T(8,128)S(1)}, f32[16,512]{0,1:T(8,128)S(1)}, u32[]{:S(2)}, u32[]{:S(2)}) %collective-permute-start.1) | collective-permute-done | bytes 32800 | tf_op jit(solution)/shard_map/ppermute | solution.py:15
  384.8 0.7 copy.25
  (12 shorter events, 0.3 us)
Async XLA Ops:
  7.2 116.9 %all-gather.2.cloned.1.call-start = ((), (), s32[]{:S(2)}) async-start(), calls=%async_computation.1 | async-start | bytes 5406720 | tf_op jit(solution)/shard_map/all_gather | solution.py:27
  7.9 367.9 %reduce-scatter.4.cloned.1.call-start = ((), (), s32[]{:S(2)}) async-start(), calls=%async_computation.2 | async-start | bytes 2162688
  124.1 116.6 %collective-permute-start = (bf16[1,5120,512]{2,1,0:T(8,128)(2,1)}, bf16[1,5120,512]{2,1,0:T(8,128)(2,1)}, u32[]{:S(2)}, u32[]{:S(2)}) collective-permute-start(bf16[1,5120,512]{2,1,0:T(8,128)(2,1)} %all-gather.2.cloned.1.call-done), channel_id=1, source_target_pairs={{0,32},{32,0},{64,96},{96,64},{128,160},{160,128},{192,224},{224,1... | collective-permute-start | bytes 15728648 | tf_op jit(solution)/shard_map/ppermute | solution.py:15
  241.4 1.4 copy-start
  244.9 0.8 copy-start.1
  376.7 8.0 %collective-permute-start.1 = (f32[16,512]{0,1:T(8,128)S(1)}, f32[16,512]{0,1:T(8,128)S(1)}, u32[]{:S(2)}, u32[]{:S(2)}) collective-permute-start(f32[16,512]{0,1:T(8,128)S(1)} %copy.29), channel_id=1, source_target_pairs={{0,32},{32,0},{64,96},{96,64},{128,160},{160,128},{192,224},{224,1... | collective-permute-start | bytes 98312 | tf_op jit(solution)/shard_map/ppermute | solution.py:15
Sparse Core Ops, SparseCore 0:
  11.1 112.8 all-gather.1
  245.0 130.6 reduce-scatter.3
where the time goes:
time: 394 us; the launch traced here: 392 us
  waiting for transfers between devices  344 us (87%)
  between operations  16.8 us (4%)
  local copies, waits for them, and re-layouts  14.9 us (4%)
  matrix products  7.02 us (2%)
  other arithmetic  5.36 us (1%)
    unnamed x3, waiting for transfers between devices  129 us
    all_gather x1, waiting for transfers between devices, body(): own_whole = lax.all_gather(child_factor, 'blk', axis=1, tiled=True)  116 us
    ppermute x2, waiting for transfers between devices, partner(): return lax.ppermute(value, axis, pairs)  98.9 us
  transfers between devices with their start and end apart: 4, of which 4 were waited for; matrix products, arithmetic and copies ran while one was open for 5% of the time, Pallas kernels for 0%

commit v1 on v0

v1 whole, which is shorter than its diff:
```python
import jax
import jax.numpy as jnp
from jax import lax
from jax.experimental import pallas as pl
from jax.experimental.pallas import tpu as pltpu
from jax.sharding import PartitionSpec as P

BS = 128
NPB = 64
NS = 40
NC = 512
SROWS = NS * BS
NZ = 4
NX = 4
NBLK = NZ * NX * 2
ROWS = SROWS // NBLK
NEAR = NX * 2
VMEM = 48 * 1024 * 1024


def ring(value, dz, dx, swap, mirrored=False):
    pairs = []
    for z in range(NZ):
        for x in range(NX):
            for c in range(2):
                s = -1 if mirrored and c else 1
                to = ((z + s * dz) % NZ * NX + (x + s * dx) % NX) * 2 + (c ^ swap)
                pairs.append(((z * NX + x) * 2 + c, to))
    return lax.ppermute(value, "blk", pairs)


def partner(value):
    pairs = [(source, source ^ 1) for source in range(lax.axis_size("front"))]
    return lax.ppermute(value, "front", pairs)


def pick_kernel(listing, rows, out):
    for i in range(NS):
        column = pl.multiple_of(listing[i] * BS, BS)
        out[:, i * BS : (i + 1) * BS] = rows[:, pl.ds(column, BS)]


def pick(listing, rows):
    return pl.pallas_call(
        pick_kernel,
        out_shape=jax.ShapeDtypeStruct((BS, SROWS), jnp.bfloat16),
        in_specs=[
            pl.BlockSpec(memory_space=pltpu.SMEM),
            pl.BlockSpec(memory_space=pltpu.VMEM),
        ],
        out_specs=pl.BlockSpec(memory_space=pltpu.VMEM),
        compiler_params=pltpu.CompilerParams(vmem_limit_bytes=VMEM),
        name="pick",
    )(listing, rows)


GROUPS = ((0,), (-1, 1), (2,))
PIECES = (0, -1, 1, 2)


def product_kernel(info, listing, rows, other_rows, *refs):
    parts = refs[: 2 * len(GROUPS)]
    own_out, other_out, turned, chosen, factor, wide, sems = refs[2 * len(GROUPS) :]
    zh, x, core = info[0], info[1], info[2]
    copies = []
    for swap in range(2):
        for g, offsets in enumerate(GROUPS):
            part = parts[swap * len(GROUPS) + g]
            side = core if swap == 0 else 1 - core
            for p, dx in enumerate(PIECES):
                for n, dz in enumerate(offsets):
                    base = ((zh + dz + NZ) % NZ * NX + (x + dx + NX) % NX) * 2 + side
                    start = pl.multiple_of(base * ROWS, 32)
                    copy = pltpu.make_async_copy(
                        part.at[pl.ds((p * len(offsets) + n) * ROWS, ROWS), :],
                        factor.at[pl.ds(start, ROWS), :],
                        sems.at[len(copies)],
                    )
                    copy.start()
                    copies.append(copy)
    for i in range(NS):
        column = pl.multiple_of(listing[i] * BS, BS)
        wide[0:BS, i * BS : (i + 1) * BS] = rows[:, pl.ds(column, BS)]
    wide[BS:, :] = other_rows[...]
    for copy in copies:
        copy.wait()
    product = jnp.dot(wide[...], factor[...], preferred_element_type=jnp.float32)
    own = jnp.where(info[3] > 0, product[:BS], 0.0)
    other = jnp.where(info[4] > 0, product[BS:], 0.0)
    own_out[...] = -own
    other_out[...] = -other
    turned[:, :BS] = own.T.astype(jnp.bfloat16)
    turned[:, BS:] = other.T.astype(jnp.bfloat16)
    for i in range(2 * NEAR):
        start = pl.multiple_of(info[8 + i] * BS, BS)
        chosen[i * BS : (i + 1) * BS, :] = factor[pl.ds(start, BS), :]


def product(info, listing, rows, other_rows, parts):
    smem = pl.BlockSpec(memory_space=pltpu.SMEM)
    vmem = pl.BlockSpec(memory_space=pltpu.VMEM)
    return pl.pallas_call(
        product_kernel,
        out_shape=[
            jax.ShapeDtypeStruct((BS, NC), jnp.float32),
            jax.ShapeDtypeStruct((BS, NC), jnp.float32),
            jax.ShapeDtypeStruct((NC, 2 * BS), jnp.bfloat16),
            jax.ShapeDtypeStruct((2 * NEAR * BS, NC), jnp.bfloat16),
        ],
        in_specs=[smem, smem, vmem, vmem]
        + [pl.BlockSpec(memory_space=pl.ANY)] * len(parts),
        out_specs=[vmem] * 4,
        scratch_shapes=[
            pltpu.VMEM((SROWS, NC), jnp.bfloat16),
            pltpu.VMEM((2 * BS, SROWS), jnp.bfloat16),
            pltpu.SemaphoreType.DMA((NBLK,)),
        ],
        compiler_params=pltpu.CompilerParams(vmem_limit_bytes=VMEM),
        name="product",
    )(info, listing, rows, other_rows, *parts)


def partial_kernel(turned, chosen, out):
    width = NC // NEAR
    left = jnp.concatenate(
        [turned[s * width : (s + 1) * width, :] for s in range(NEAR)], axis=1
    )
    total = jnp.dot(left, chosen[...], preferred_element_type=jnp.float32)
    tall = total.T
    for d in range(NBLK):
        first = tall[d * 16 : d * 16 + 8]
        second = tall[d * 16 + 8 : d * 16 + 16]
        out[d * 8 : (d + 1) * 8, :] = jnp.concatenate([first, second], axis=1)


def partial(turned, chosen):
    vmem = pl.BlockSpec(memory_space=pltpu.VMEM)
    return pl.pallas_call(
        partial_kernel,
        out_shape=jax.ShapeDtypeStruct((NBLK * 8, BS), jnp.float32),
        in_specs=[vmem, vmem],
        out_specs=vmem,
        compiler_params=pltpu.CompilerParams(vmem_limit_bytes=VMEM),
        name="partial",
    )(turned, chosen)


def total_kernel(terms, diagonal, out):
    half = BS // 2
    for j in range(NEAR):
        tile = terms[j * 8 : (j + 1) * 8, :]
        for z in range(1, NZ):
            at = (z * NEAR + j) * 8
            tile = tile + terms[at : at + 8, :]
        columns = slice(j * half, (j + 1) * half)
        out[0:8, columns] = diagonal[0:8, columns] + tile[:, :half]
        out[8:16, columns] = diagonal[8:16, columns] + tile[:, half:]


def total(terms, diagonal):
    vmem = pl.BlockSpec(memory_space=pltpu.VMEM)
    return pl.pallas_call(
        total_kernel,
        out_shape=jax.ShapeDtypeStruct((NC // NBLK, NC), jnp.float32),
        in_specs=[vmem, vmem],
        out_specs=vmem,
        name="total",
    )(terms, diagonal)


def around_x(value, core):
    right = ring(value, 0, 1, 0)
    left = ring(value, 0, -1, 0)
    far = ring(jnp.where(core == 0, right, left), 0, 1, 0, mirrored=True)
    pieces = jnp.concatenate([value, right, left, far], axis=0)
    return pieces, ring(pieces, 0, 0, 1)


def body(parent_inverse, child_factor, child_diagonal, structure):
    blk = lax.axis_index("blk")
    front = lax.axis_index("front")
    half = front % 2
    zh, x, core = blk // NEAR, blk // 2 % NX, blk % 2
    lists = lax.dynamic_slice_in_dim(structure, front - half, 2, 0)
    listing = lax.dynamic_index_in_dim(lists, half, 0, keepdims=False)
    other_listing = lax.dynamic_index_in_dim(lists, 1 - half, 0, keepdims=False)
    rows = parent_inverse[0]
    mine = child_factor[0]

    up = ring(mine, 1, 0, 0)
    down = ring(mine, -1, 0, 0)
    other_rows = partner(pick(other_listing, rows))
    across = ring(jnp.where(core == 0, up, down), 1, 0, 0, mirrored=True)
    near, near_swapped = around_x(mine, core)
    sides, sides_swapped = around_x(jnp.concatenate([up, down], axis=0), core)
    far, far_swapped = around_x(across, core)

    near_at = zh * NEAR + jnp.arange(NEAR)
    blocks = jnp.stack(
        [half * (NPB // 2) + near_at, (1 - half) * (NPB // 2) + near_at], axis=1
    ).reshape(-1)
    position = jnp.sum((listing[None, :] < blocks[:, None]).astype(jnp.int32), axis=1)
    position = jnp.minimum(position, NS - 1)
    wanted = jnp.stack([half * (NPB // 2) + blk, (1 - half) * (NPB // 2) + blk])
    member = jnp.any(listing[None, :] == wanted[:, None], axis=1).astype(jnp.int32)
    info = jnp.concatenate(
        [jnp.stack([zh, x, core]), member, jnp.zeros((3,), jnp.int32), position]
    )
    own_out, other_out, turned, chosen = product(
        info,
        listing,
        rows,
        other_rows,
        (near, sides, far, near_swapped, sides_swapped, far_swapped),
    )
    second = partner(other_out)
    groups = [[z * NEAR + i for i in range(NEAR)] for z in range(NZ)]
    turned = lax.all_to_all(
        turned, "blk", 0, 0, axis_index_groups=groups, tiled=True
    )
    terms = lax.all_to_all(partial(turned, chosen), "blk", 0, 0, tiled=True)
    inverse = total(terms, child_diagonal[0])
    placed = jnp.stack([own_out, second], axis=1)
    return placed[None], inverse[None]


def solution(mesh):
    in_specs = (P("front", "blk", None), P("front", "blk", None), P("front", "blk", None), P())
    out_specs = (P("front", "blk", None, None), P("front", "blk", None))
    return jax.shard_map(body, mesh=mesh, in_specs=in_specs, out_specs=out_specs, check_vma=False)
```

time: 394 us -> 173 us (0.44)
  waiting for transfers between devices: 344 us -> 31.2 us
  starting transfers between devices: 3.91 us -> 102 us
  between operations: 16.8 us -> 1.01 us
  Pallas kernels: 0 us -> 14.4 us
  blocking collectives: 0 us -> 9.28 us
  matrix products: 7.02 us -> 0 us
  local copies, waits for them, and re-layouts: 14.9 us -> 9.78 us
    unnamed x3 -> x0, waiting for transfers between devices: 129 us -> none
    all_gather x1 -> x0, waiting for transfers between devices: 116 us -> none  [body(): own_whole = lax.all_gather(child_factor, 'blk', axis=1, tiled=True)]
    ppermute x2 -> x17, starting transfers between devices: 3.83 us -> 90.6 us  [the longest x15 86.7 us: ring(): return lax.ppermute(value, 'blk', pairs)]
    ppermute x2 -> x17, waiting for transfers between devices: 98.9 us -> 27.5 us  [the longest x15 18.9 us: ring(): return lax.ppermute(value, 'blk', pairs)]
    pallas_call x0 -> x4, Pallas kernels: none -> 14.4 us  [the longest x1 9.49 us: product(): pl.pallas_call(product_kernel, out_shape=[jax.ShapeDtypeStruct((BS, NC),...]
    all_to_all x0 -> x1, starting transfers between devices: none -> 11.5 us  [body(): terms = lax.all_to_all(partial(turned, chosen), 'blk', 0, 0, tiled=True)]
    all_to_all x0 -> x1, blocking collectives: none -> 9.28 us  [body(): lax.all_to_all(turned, 'blk', 0, 0, axis_index_groups=groups, tiled=True)]
    another operation x5 -> x2, local copies, waits for them, and re-layouts: 7.24 us -> 0.08 us  [the longest x1 0.08 us: body(): jnp.stack([half * (NPB // 2) + near_at, (1 - half) * (NPB // 2) + near_at...]
  transfers between devices with their start and end apart: 4 -> 18, of which waited for: 4 -> 5; matrix products, arithmetic and copies ran while one was open for 5% -> 5% of each run, Pallas kernels for 0% -> 1%
where the time goes in v1:
time: 173 us; the launch traced here: 172 us
  starting transfers between devices  102 us (59%)
  waiting for transfers between devices  31.2 us (18%)
  Pallas kernels  14.4 us (8%)
  local copies, waits for them, and re-layouts  9.78 us (6%)
  blocking collectives  9.28 us (5%)
  other arithmetic  4.27 us (2%)
    ppermute x15, starting transfers between devices, ring(): return lax.ppermute(value, 'blk', pairs)  86.7 us
    ppermute x15, waiting for transfers between devices, ring(): return lax.ppermute(value, 'blk', pairs)  18.9 us
    all_to_all x1, starting transfers between devices, body(): terms = lax.all_to_all(partial(turned, chosen), 'blk', 0, 0, tiled=True)  11.5 us
    pallas_call x1, Pallas kernels, product(): pl.pallas_call(product_kernel, out_shape=[jax.ShapeDtypeStruct((BS, NC),...  9.49 us
    all_to_all x1, blocking collectives, body(): lax.all_to_all(turned, 'blk', 0, 0, axis_index_groups=groups, tiled=True)  9.28 us
    ppermute x2, waiting for transfers between devices, partner(): return lax.ppermute(value, 'front', pairs)  8.56 us
    unnamed x17, local copies, waits for them, and re-layouts  7.14 us
    ppermute x2, starting transfers between devices, partner(): return lax.ppermute(value, 'front', pairs)  3.83 us
  transfers between devices with their start and end apart: 18, of which 5 were waited for; matrix products, arithmetic and copies ran while one was open for 5% of the time, Pallas kernels for 1%

profile of v1, /device:TPU:1, one launch (start us, length us, event | category | flops | bytes accessed | tf_op | source)
XLA Modules:
  0.0 172.0 jit_solution(7195357746017577735)
XLA Ops:
  0.6 9.8 %collective-permute-start.4 = (bf16[160,512]{1,0:T(8,128)(2,1)}, bf16[160,512]{1,0:T(8,128)(2,1)S(1)}, u32[]{:S(2)}, u32[]{:S(2)}) collective-permute-start(bf16[160,512]{1,0:T(8,128)(2,1)} %bitcast.28), channel_id=1, source_target_pairs={{0,8},{1,9},{2,10},{3,11},{4,12},{5,13},{6,14},{7,15},{8,16},{9,17... | collective-permute-start | bytes 491528 | tf_op jit(solution)/shard_map/ppermute | solution.py:29
  10.4 5.6 %collective-permute-start.5 = (bf16[160,512]{1,0:T(8,128)(2,1)}, bf16[160,512]{1,0:T(8,128)(2,1)S(1)}, u32[]{:S(2)}, u32[]{:S(2)}) collective-permute-start(bf16[160,512]{1,0:T(8,128)(2,1)} %bitcast.29), channel_id=1, source_target_pairs={{0,24},{1,25},{2,26},{3,27},{4,28},{5,29},{6,30},{7,31},{8,0},{9,1... | collective-permute-start | bytes 491528 | tf_op jit(solution)/shard_map/ppermute | solution.py:29
  16.0 1.8 %collective-permute-done.4 = bf16[160,512]{1,0:T(8,128)(2,1)S(1)} collective-permute-done((bf16[160,512]{1,0:T(8,128)(2,1)}, bf16[160,512]{1,0:T(8,128)(2,1)S(1)}, u32[]{:S(2)}, u32[]{:S(2)}) %collective-permute-start.4) | collective-permute-done | bytes 163872 | tf_op jit(solution)/shard_map/ppermute | solution.py:29
  18.5 15.7 %collective-permute-done.5 = bf16[160,512]{1,0:T(8,128)(2,1)S(1)} collective-permute-done((bf16[160,512]{1,0:T(8,128)(2,1)}, bf16[160,512]{1,0:T(8,128)(2,1)S(1)}, u32[]{:S(2)}, u32[]{:S(2)}) %collective-permute-start.5) | collective-permute-done | bytes 163872 | tf_op jit(solution)/shard_map/ppermute | solution.py:29
  35.0 3.1 %collective-permute-start.6 = (bf16[320,512]{1,0:T(8,128)(2,1)}, bf16[320,512]{1,0:T(8,128)(2,1)S(1)}, u32[]{:S(2)}, u32[]{:S(2)}) collective-permute-start(bf16[320,512]{1,0:T(8,128)(2,1)} %get-tuple-element.24), channel_id=1, source_target_pairs={{0,2},{1,3},{2,4},{3,5},{4,6},{5,7},{6,0},{7,1},{8,10},{9,11},{10,... | collective-permute-start | bytes 983048 | tf_op jit(solution)/shard_map/ppermute | solution.py:29
  38.1 3.4 %collective-permute-start.7 = (bf16[320,512]{1,0:T(8,128)(2,1)}, bf16[320,512]{1,0:T(8,128)(2,1)}, u32[]{:S(2)}, u32[]{:S(2)}) collective-permute-start(bf16[320,512]{1,0:T(8,128)(2,1)} %get-tuple-element.24), channel_id=1, source_target_pairs={{0,6},{1,7},{2,0},{3,1},{4,2},{5,3},{6,4},{7,5},{8,14},{9,15},{10,... | collective-permute-start | bytes 983048 | tf_op jit(solution)/shard_map/ppermute | solution.py:29
  41.5 3.2 %collective-permute-start.2 = (bf16[160,512]{1,0:T(8,128)(2,1)S(1)}, bf16[160,512]{1,0:T(8,128)(2,1)S(1)}, u32[]{:S(2)}, u32[]{:S(2)}) collective-permute-start(bf16[160,512]{1,0:T(8,128)(2,1)S(1)} %bitcast.31), channel_id=1, source_target_pairs={{0,6},{1,7},{2,0},{3,1},{4,2},{5,3},{6,4},{7,5},{8,14},{9,15},{10,... | collective-permute-start | bytes 491528 | tf_op jit(solution)/shard_map/ppermute | solution.py:29
  44.7 2.1 %collective-permute-start.1 = (bf16[160,512]{1,0:T(8,128)(2,1)S(1)}, bf16[160,512]{1,0:T(8,128)(2,1)S(1)}, u32[]{:S(2)}, u32[]{:S(2)}) collective-permute-start(bf16[160,512]{1,0:T(8,128)(2,1)S(1)} %bitcast.32), channel_id=1, source_target_pairs={{0,2},{1,3},{2,4},{3,5},{4,6},{5,7},{6,0},{7,1},{8,10},{9,11},{10,... | collective-permute-start | bytes 491528 | tf_op jit(solution)/shard_map/ppermute | solution.py:29
  47.6 1.6 copy-done
  49.2 2.0 %pick.1 = bf16[128,5120]{1,0:T(8,128)(2,1)} custom-call(s32[40]{0:T(128)S(1)} %get-tuple-element.27.listing, bf16[128,8192]{1,0:T(8,128)(2,1)S(1)} %bitcast.22), custom_call_target="tpu_custom_call" | custom-call | tf_op jit(solution)/shard_map/pick/pallas_call | solution.py:44
  51.2 1.9 %collective-permute-start = (bf16[128,5120]{1,0:T(8,128)(2,1)}, bf16[128,5120]{1,0:T(8,128)(2,1)S(1)}, u32[]{:S(2)}, u32[]{:S(2)}) collective-permute-start(bf16[128,5120]{1,0:T(8,128)(2,1)} %pick.1), channel_id=1, source_target_pairs={{0,32},{32,0},{64,96},{96,64},{128,160},{160,128},{192,224},{224,1... | collective-permute-start | bytes 3932168 | tf_op jit(solution)/shard_map/ppermute | solution.py:34
  53.1 4.0 %collective-permute-start.9 = (bf16[160,512]{1,0:T(8,128)(2,1)}, bf16[160,512]{1,0:T(8,128)(2,1)S(1)}, u32[]{:S(2)}, u32[]{:S(2)}) collective-permute-start(bf16[160,512]{1,0:T(8,128)(2,1)} %get-tuple-element.22), channel_id=1, source_target_pairs={{0,8},{1,25},{2,10},{3,27},{4,12},{5,29},{6,14},{7,31},{8,16},{9,1... | collective-permute-start | bytes 491528 | tf_op jit(solution)/shard_map/ppermute | solution.py:29
  58.3 4.4 %collective-permute-start.8 = (bf16[320,512]{1,0:T(8,128)(2,1)S(1)}, bf16[320,512]{1,0:T(8,128)(2,1)S(1)}, u32[]{:S(2)}, u32[]{:S(2)}) collective-permute-start(bf16[320,512]{1,0:T(8,128)(2,1)S(1)} %get-tuple-element.18), channel_id=1, source_target_pairs={{0,2},{1,7},{2,4},{3,1},{4,6},{5,3},{6,0},{7,5},{8,10},{9,15},{10,... | collective-permute-start | bytes 983048 | tf_op jit(solution)/shard_map/ppermute | solution.py:29
  62.8 1.9 %collective-permute-start.3 = (bf16[160,512]{1,0:T(8,128)(2,1)S(1)}, bf16[160,512]{1,0:T(8,128)(2,1)}, u32[]{:S(2)}, u32[]{:S(2)}) collective-permute-start(bf16[160,512]{1,0:T(8,128)(2,1)S(1)} %broadcast_select_fusion.3), channel_id=1, source_target_pairs={{0,2},{1,7},{2,4},{3,1},{4,6},{5,3},{6,0},{7,5},{8,10},{9,15},{10,... | collective-permute-start | bytes 491528 | tf_op jit(solution)/shard_map/ppermute | solution.py:29
  64.8 3.1 %collective-permute-start.11 = (bf16[160,512]{1,0:T(8,128)(2,1)S(1)}, bf16[160,512]{1,0:T(8,128)(2,1)S(1)}, u32[]{:S(2)}, u32[]{:S(2)}) collective-permute-start(bf16[160,512]{1,0:T(8,128)(2,1)S(1)} %collective-permute-done.9), channel_id=1, source_target_pairs={{0,6},{1,7},{2,0},{3,1},{4,2},{5,3},{6,4},{7,5},{8,14},{9,15},{10,... | collective-permute-start | bytes 491528 | tf_op jit(solution)/shard_map/ppermute | solution.py:29
  67.9 2.2 %collective-permute-start.10 = (bf16[160,512]{1,0:T(8,128)(2,1)S(1)}, bf16[160,512]{1,0:T(8,128)(2,1)S(1)}, u32[]{:S(2)}, u32[]{:S(2)}) collective-permute-start(bf16[160,512]{1,0:T(8,128)(2,1)S(1)} %collective-permute-done.9), channel_id=1, source_target_pairs={{0,2},{1,3},{2,4},{3,5},{4,6},{5,7},{6,0},{7,1},{8,10},{9,11},{10,... | collective-permute-start | bytes 491528 | tf_op jit(solution)/shard_map/ppermute | solution.py:29
  70.8 30.7 %collective-permute-start.14 = (bf16[1280,512]{1,0:T(8,128)(2,1)S(1)}, bf16[1280,512]{1,0:T(8,128)(2,1)}, u32[]{:S(2)}, u32[]{:S(2)}) collective-permute-start(bf16[1280,512]{1,0:T(8,128)(2,1)S(1)} %constant_dynamic-update-slice_fusion.2.refs_1_), channel_id=1, source_target_pairs={{0,1},{1,0},{2,3},{3,2},{4,5},{5,4},{6,7},{7,6},{8,9},{9,8},{10,11... | collective-permute-start | bytes 3932168 | tf_op jit(solution)/shard_map/ppermute | solution.py:29
  103.0 4.8 %collective-permute-start.12 = (bf16[160,512]{1,0:T(8,128)(2,1)}, bf16[160,512]{1,0:T(8,128)(2,1)}, u32[]{:S(2)}, u32[]{:S(2)}) collective-permute-start(bf16[160,512]{1,0:T(8,128)(2,1)} %get-tuple-element.20), channel_id=1, source_target_pairs={{0,2},{1,7},{2,4},{3,1},{4,6},{5,3},{6,0},{7,5},{8,10},{9,15},{10,... | collective-permute-start | bytes 491528 | tf_op jit(solution)/shard_map/ppermute | solution.py:29
  109.0 2.8 %collective-permute-start.13 = (bf16[640,512]{1,0:T(8,128)(2,1)S(1)}, bf16[640,512]{1,0:T(8,128)(2,1)}, u32[]{:S(2)}, u32[]{:S(2)}) collective-permute-start(bf16[640,512]{1,0:T(8,128)(2,1)S(1)} %pad_maximum_fusion.refs_0_), channel_id=1, source_target_pairs={{0,1},{1,0},{2,3},{3,2},{4,5},{5,4},{6,7},{7,6},{8,9},{9,8},{10,11... | collective-permute-start | bytes 1966088 | tf_op jit(solution)/shard_map/ppermute | solution.py:29
  111.8 1.6 constant_dynamic-update-slice_fusion.7.refs_2_
  113.5 5.6 %collective-permute-start.15 = (bf16[640,512]{1,0:T(8,128)(2,1)}, bf16[640,512]{1,0:T(8,128)(2,1)}, u32[]{:S(2)}, u32[]{:S(2)}) collective-permute-start(bf16[640,512]{1,0:T(8,128)(2,1)} %constant_dynamic-update-slice_fusion.7.refs_2_), channel_id=1, source_target_pairs={{0,1},{1,0},{2,3},{3,2},{4,5},{5,4},{6,7},{7,6},{8,9},{9,8},{10,11... | collective-permute-start | bytes 1966088 | tf_op jit(solution)/shard_map/ppermute | solution.py:29
  119.7 1.4 collective-permute-done.15.refs_5_
  121.1 9.5 %product.1 = (f32[128,512]{1,0:T(8,128)S(1)}, f32[128,512]{1,0:T(8,128)S(1)}, bf16[512,256]{1,0:T(8,128)(2,1)S(1)}, bf16[2048,512]{1,0:T(8,128)(2,1)}) custom-call(s32[24]{0:T(128)S(1)} %concatenate.16.info, s32[40]{0:T(128)S(1)} %get-tuple-element.28.listing, bf16[128,8192]{1,0:T(8,128)(2,1)} %bitcast.21, ...), custom_call_target="tpu_custom_call" | custom-call | tf_op jit(solution)/shard_map/product/pallas_call | solution.py:102
  130.6 9.3 %all_to_all.22 = bf16[8,64,256]{2,1,0:T(8,128)(2,1)S(1)} all-to-all(bf16[8,64,256]{2,1,0:T(8,128)(2,1)S(1)} %bitcast.24), channel_id=1, replica_groups={{0,1,2,3,4,5,6,7},{8,9,10,11,12,13,14,15},{16,17,18,19,20,21,22,23},{24..., dimensions={0} | all-to-all | bytes 524288 | tf_op jit(solution)/shard_map/all_to_all | solution.py:218
  139.9 1.6 copy-done.1
  141.5 1.3 partial.1
  142.8 11.5 %all-to-all-start.1 = ((f32[32,8,128]{2,1,0:T(8,128)}), f32[32,8,128]{2,1,0:T(8,128)S(1)}, u32[]{:S(2)}, u32[]{:S(2)}) async-start(f32[32,8,128]{2,1,0:T(8,128)} %bitcast.14), calls=%async_computation.1 | async-start | bytes 262144 | tf_op jit(solution)/shard_map/all_to_all | solution.py:221
  154.3 1.9 %collective-permute-start.16 = (f32[128,512]{1,0:T(8,128)}, f32[128,512]{1,0:T(8,128)S(1)}, u32[]{:S(2)}, u32[]{:S(2)}) collective-permute-start(f32[128,512]{1,0:T(8,128)} %copy-done.2), channel_id=1, source_target_pairs={{0,32},{32,0},{64,96},{96,64},{128,160},{160,128},{192,224},{224,1... | collective-permute-start | bytes 786440 | tf_op jit(solution)/shard_map/ppermute | solution.py:34
  156.2 8.6 %collective-permute-done.16 = f32[128,512]{1,0:T(8,128)S(1)} collective-permute-done((f32[128,512]{1,0:T(8,128)}, f32[128,512]{1,0:T(8,128)S(1)}, u32[]{:S(2)}, u32[]{:S(2)}) %collective-permute-start.16) | collective-permute-done | bytes 262176 | tf_op jit(solution)/shard_map/ppermute | solution.py:34
  164.8 1.2 copy.11
  166.0 3.7 %all-to-all-done.1 = f32[32,8,128]{2,1,0:T(8,128)S(1)} async-done(((f32[32,8,128]{2,1,0:T(8,128)}), f32[32,8,128]{2,1,0:T(8,128)S(1)}, u32[]{:S(2)}, u32[]{:S(2)}) %all-to-all-start.1) | async-done | bytes 131104 | tf_op jit(solution)/shard_map/all_to_all | solution.py:221
  170.4 1.6 total.1
  (46 shorter events, 8.1 us)
Async XLA Ops:
  0.6 40.9 %copy-start.5 = (bf16[1,160,512]{2,1,0:T(8,128)(2,1)S(1)}, bf16[1,160,512]{2,1,0:T(8,128)(2,1)}, u32[]{:S(2)}) copy-start(bf16[1,160,512]{2,1,0:T(8,128)(2,1)} %param.5) | copy-start | bytes 491524
  0.6 17.2 %collective-permute-start.4 = (bf16[160,512]{1,0:T(8,128)(2,1)}, bf16[160,512]{1,0:T(8,128)(2,1)S(1)}, u32[]{:S(2)}, u32[]{:S(2)}) collective-permute-start(bf16[160,512]{1,0:T(8,128)(2,1)} %bitcast.28), channel_id=1, source_target_pairs={{0,8},{1,9},{2,10},{3,11},{4,12},{5,13},{6,14},{7,15},{8,16},{9,17... | collective-permute-start | bytes 491528 | tf_op jit(solution)/shard_map/ppermute | solution.py:29
  10.4 23.8 %collective-permute-start.5 = (bf16[160,512]{1,0:T(8,128)(2,1)}, bf16[160,512]{1,0:T(8,128)(2,1)S(1)}, u32[]{:S(2)}, u32[]{:S(2)}) collective-permute-start(bf16[160,512]{1,0:T(8,128)(2,1)} %bitcast.29), channel_id=1, source_target_pairs={{0,24},{1,25},{2,26},{3,27},{4,28},{5,29},{6,30},{7,31},{8,0},{9,1... | collective-permute-start | bytes 491528 | tf_op jit(solution)/shard_map/ppermute | solution.py:29
  35.0 18.1 %collective-permute-start.6 = (bf16[320,512]{1,0:T(8,128)(2,1)}, bf16[320,512]{1,0:T(8,128)(2,1)S(1)}, u32[]{:S(2)}, u32[]{:S(2)}) collective-permute-start(bf16[320,512]{1,0:T(8,128)(2,1)} %get-tuple-element.24), channel_id=1, source_target_pairs={{0,2},{1,3},{2,4},{3,5},{4,6},{5,7},{6,0},{7,1},{8,10},{9,11},{10,... | collective-permute-start | bytes 983048 | tf_op jit(solution)/shard_map/ppermute | solution.py:29
  38.1 19.1 %collective-permute-start.7 = (bf16[320,512]{1,0:T(8,128)(2,1)}, bf16[320,512]{1,0:T(8,128)(2,1)}, u32[]{:S(2)}, u32[]{:S(2)}) collective-permute-start(bf16[320,512]{1,0:T(8,128)(2,1)} %get-tuple-element.24), channel_id=1, source_target_pairs={{0,6},{1,7},{2,0},{3,1},{4,2},{5,3},{6,4},{7,5},{8,14},{9,15},{10,... | collective-permute-start | bytes 983048 | tf_op jit(solution)/shard_map/ppermute | solution.py:29
  41.5 21.2 %collective-permute-start.2 = (bf16[160,512]{1,0:T(8,128)(2,1)S(1)}, bf16[160,512]{1,0:T(8,128)(2,1)S(1)}, u32[]{:S(2)}, u32[]{:S(2)}) collective-permute-start(bf16[160,512]{1,0:T(8,128)(2,1)S(1)} %bitcast.31), channel_id=1, source_target_pairs={{0,6},{1,7},{2,0},{3,1},{4,2},{5,3},{6,4},{7,5},{8,14},{9,15},{10,... | collective-permute-start | bytes 491528 | tf_op jit(solution)/shard_map/ppermute | solution.py:29
  44.7 18.0 %collective-permute-start.1 = (bf16[160,512]{1,0:T(8,128)(2,1)S(1)}, bf16[160,512]{1,0:T(8,128)(2,1)S(1)}, u32[]{:S(2)}, u32[]{:S(2)}) collective-permute-start(bf16[160,512]{1,0:T(8,128)(2,1)S(1)} %bitcast.32), channel_id=1, source_target_pairs={{0,2},{1,3},{2,4},{3,5},{4,6},{5,7},{6,0},{7,1},{8,10},{9,11},{10,... | collective-permute-start | bytes 491528 | tf_op jit(solution)/shard_map/ppermute | solution.py:29
  47.6 1.6 copy-start
  51.2 68.5 %collective-permute-start = (bf16[128,5120]{1,0:T(8,128)(2,1)}, bf16[128,5120]{1,0:T(8,128)(2,1)S(1)}, u32[]{:S(2)}, u32[]{:S(2)}) collective-permute-start(bf16[128,5120]{1,0:T(8,128)(2,1)} %pick.1), channel_id=1, source_target_pairs={{0,32},{32,0},{64,96},{96,64},{128,160},{160,128},{192,224},{224,1... | collective-permute-start | bytes 3932168 | tf_op jit(solution)/shard_map/ppermute | solution.py:34
  53.1 11.6 %collective-permute-start.9 = (bf16[160,512]{1,0:T(8,128)(2,1)}, bf16[160,512]{1,0:T(8,128)(2,1)S(1)}, u32[]{:S(2)}, u32[]{:S(2)}) collective-permute-start(bf16[160,512]{1,0:T(8,128)(2,1)} %get-tuple-element.22), channel_id=1, source_target_pairs={{0,8},{1,25},{2,10},{3,27},{4,12},{5,29},{6,14},{7,31},{8,16},{9,1... | collective-permute-start | bytes 491528 | tf_op jit(solution)/shard_map/ppermute | solution.py:29
  58.3 12.4 %collective-permute-start.8 = (bf16[320,512]{1,0:T(8,128)(2,1)S(1)}, bf16[320,512]{1,0:T(8,128)(2,1)S(1)}, u32[]{:S(2)}, u32[]{:S(2)}) collective-permute-start(bf16[320,512]{1,0:T(8,128)(2,1)S(1)} %get-tuple-element.18), channel_id=1, source_target_pairs={{0,2},{1,7},{2,4},{3,1},{4,6},{5,3},{6,0},{7,5},{8,10},{9,15},{10,... | collective-permute-start | bytes 983048 | tf_op jit(solution)/shard_map/ppermute | solution.py:29
  62.8 45.1 %copy-start.3 = (bf16[160,512]{1,0:T(8,128)(2,1)}, bf16[160,512]{1,0:T(8,128)(2,1)S(1)}, u32[]{:S(2)}) copy-start(bf16[160,512]{1,0:T(8,128)(2,1)S(1)} %collective-permute-done.1) | copy-start | bytes 491524
  62.8 45.1 %collective-permute-start.3 = (bf16[160,512]{1,0:T(8,128)(2,1)S(1)}, bf16[160,512]{1,0:T(8,128)(2,1)}, u32[]{:S(2)}, u32[]{:S(2)}) collective-permute-start(bf16[160,512]{1,0:T(8,128)(2,1)S(1)} %broadcast_select_fusion.3), channel_id=1, source_target_pairs={{0,2},{1,7},{2,4},{3,1},{4,6},{5,3},{6,0},{7,5},{8,10},{9,15},{10,... | collective-permute-start | bytes 491528 | tf_op jit(solution)/shard_map/ppermute | solution.py:29
  64.8 37.4 %collective-permute-start.11 = (bf16[160,512]{1,0:T(8,128)(2,1)S(1)}, bf16[160,512]{1,0:T(8,128)(2,1)S(1)}, u32[]{:S(2)}, u32[]{:S(2)}) collective-permute-start(bf16[160,512]{1,0:T(8,128)(2,1)S(1)} %collective-permute-done.9), channel_id=1, source_target_pairs={{0,6},{1,7},{2,0},{3,1},{4,2},{5,3},{6,4},{7,5},{8,14},{9,15},{10,... | collective-permute-start | bytes 491528 | tf_op jit(solution)/shard_map/ppermute | solution.py:29
  67.9 33.6 %collective-permute-start.10 = (bf16[160,512]{1,0:T(8,128)(2,1)S(1)}, bf16[160,512]{1,0:T(8,128)(2,1)S(1)}, u32[]{:S(2)}, u32[]{:S(2)}) collective-permute-start(bf16[160,512]{1,0:T(8,128)(2,1)S(1)} %collective-permute-done.9), channel_id=1, source_target_pairs={{0,2},{1,3},{2,4},{3,5},{4,6},{5,7},{6,0},{7,1},{8,10},{9,11},{10,... | collective-permute-start | bytes 491528 | tf_op jit(solution)/shard_map/ppermute | solution.py:29
  70.8 50.3 %collective-permute-start.14 = (bf16[1280,512]{1,0:T(8,128)(2,1)S(1)}, bf16[1280,512]{1,0:T(8,128)(2,1)}, u32[]{:S(2)}, u32[]{:S(2)}) collective-permute-start(bf16[1280,512]{1,0:T(8,128)(2,1)S(1)} %constant_dynamic-update-slice_fusion.2.refs_1_), channel_id=1, source_target_pairs={{0,1},{1,0},{2,3},{3,2},{4,5},{5,4},{6,7},{7,6},{8,9},{9,8},{10,11... | collective-permute-start | bytes 3932168 | tf_op jit(solution)/shard_map/ppermute | solution.py:29
  103.0 8.9 %collective-permute-start.12 = (bf16[160,512]{1,0:T(8,128)(2,1)}, bf16[160,512]{1,0:T(8,128)(2,1)}, u32[]{:S(2)}, u32[]{:S(2)}) collective-permute-start(bf16[160,512]{1,0:T(8,128)(2,1)} %get-tuple-element.20), channel_id=1, source_target_pairs={{0,2},{1,7},{2,4},{3,1},{4,6},{5,3},{6,0},{7,5},{8,10},{9,15},{10,... | collective-permute-start | bytes 491528 | tf_op jit(solution)/shard_map/ppermute | solution.py:29
  109.0 10.7 %collective-permute-start.13 = (bf16[640,512]{1,0:T(8,128)(2,1)S(1)}, bf16[640,512]{1,0:T(8,128)(2,1)}, u32[]{:S(2)}, u32[]{:S(2)}) collective-permute-start(bf16[640,512]{1,0:T(8,128)(2,1)S(1)} %pad_maximum_fusion.refs_0_), channel_id=1, source_target_pairs={{0,1},{1,0},{2,3},{3,2},{4,5},{5,4},{6,7},{7,6},{8,9},{9,8},{10,11... | collective-permute-start | bytes 1966088 | tf_op jit(solution)/shard_map/ppermute | solution.py:29
  113.5 7.6 %collective-permute-start.15 = (bf16[640,512]{1,0:T(8,128)(2,1)}, bf16[640,512]{1,0:T(8,128)(2,1)}, u32[]{:S(2)}, u32[]{:S(2)}) collective-permute-start(bf16[640,512]{1,0:T(8,128)(2,1)} %constant_dynamic-update-slice_fusion.7.refs_2_), channel_id=1, source_target_pairs={{0,1},{1,0},{2,3},{3,2},{4,5},{5,4},{6,7},{7,6},{8,9},{9,8},{10,11... | collective-permute-start | bytes 1966088 | tf_op jit(solution)/shard_map/ppermute | solution.py:29
  130.6 12.2 %copy-start.2 = (f32[128,512]{1,0:T(8,128)}, f32[128,512]{1,0:T(8,128)S(1)}, u32[]{:S(2)}) copy-start(f32[128,512]{1,0:T(8,128)S(1)} %get-tuple-element.7) | copy-start | bytes 786436
  139.9 1.6 copy-start.1
  142.8 26.9 %all-to-all-start.1 = ((f32[32,8,128]{2,1,0:T(8,128)}), f32[32,8,128]{2,1,0:T(8,128)S(1)}, u32[]{:S(2)}, u32[]{:S(2)}) async-start(f32[32,8,128]{2,1,0:T(8,128)} %bitcast.14), calls=%async_computation.1 | async-start | bytes 262144 | tf_op jit(solution)/shard_map/all_to_all | solution.py:221
  154.3 10.5 %collective-permute-start.16 = (f32[128,512]{1,0:T(8,128)}, f32[128,512]{1,0:T(8,128)S(1)}, u32[]{:S(2)}, u32[]{:S(2)}) collective-permute-start(f32[128,512]{1,0:T(8,128)} %copy-done.2), channel_id=1, source_target_pairs={{0,32},{32,0},{64,96},{96,64},{128,160},{160,128},{192,224},{224,1... | collective-permute-start | bytes 786440 | tf_op jit(solution)/shard_map/ppermute | solution.py:34
  169.7 0.7 copy-start.4

commit v2 on v1

v2 whole, which is shorter than its diff:
```python
import jax
import jax.numpy as jnp
from jax import lax
from jax.experimental import pallas as pl
from jax.experimental.pallas import tpu as pltpu
from jax.sharding import PartitionSpec as P

BS = 128
NPB = 64
NS = 40
NC = 512
SROWS = NS * BS
NZ = 4
NX = 4
NBLK = NZ * NX * 2
ROWS = SROWS // NBLK
NEAR = NX * 2
VMEM = 32 * 1024 * 1024


def ring(value, dz, dx, swap, mirrored=False):
    pairs = []
    for z in range(NZ):
        for x in range(NX):
            for c in range(2):
                s = -1 if mirrored and c else 1
                to = ((z + s * dz) % NZ * NX + (x + s * dx) % NX) * 2 + (c ^ swap)
                pairs.append(((z * NX + x) * 2 + c, to))
    return lax.ppermute(value, "blk", pairs)


def partner(value):
    pairs = [(source, source ^ 1) for source in range(lax.axis_size("front"))]
    return lax.ppermute(value, "front", pairs)


SENT = (40,)


def pick_kernel(lists, rows, own, *others):
    for i in range(NS):
        columns = pl.ds(pl.multiple_of(lists[0, i] * BS, BS), BS)
        own[:, i * BS : (i + 1) * BS] = rows[:, columns]
    i = 0
    for n, count in enumerate(SENT):
        for at in range(count):
            columns = pl.ds(pl.multiple_of(lists[1, i] * BS, BS), BS)
            others[n][:, at * BS : (at + 1) * BS] = rows[:, columns]
            i += 1


def pick(lists, rows):
    vmem = pl.BlockSpec(memory_space=pltpu.VMEM)
    return pl.pallas_call(
        pick_kernel,
        out_shape=[pltpu.VMEM((BS, SROWS), jnp.bfloat16)]
        + [jax.ShapeDtypeStruct((BS, count * BS), jnp.bfloat16) for count in SENT],
        in_specs=[pl.BlockSpec(memory_space=pltpu.SMEM), vmem],
        out_specs=[vmem] * (1 + len(SENT)),
        compiler_params=pltpu.CompilerParams(vmem_limit_bytes=VMEM),
        name="pick",
    )(lists, rows)


EARLY = tuple((0, dx) for dx in (0, -1, 1)) + tuple(
    (dz, dx) for dx in (0, -1, 1) for dz in (-1, 1, 2)
)
LATE = tuple((dz, 2) for dz in (0, -1, 1, 2))
ZROWS = SROWS // NZ


def fetch(info, factor, sems, sources):
    zh, x, core = info[0], info[1], info[2]
    copies = {dz: [] for dz in (0, -1, 1, 2)}
    count = 0
    for part, offsets, swapped in sources:
        side = 1 - core if swapped else core
        for p, (dz, dx) in enumerate(offsets):
            base = ((zh + dz + NZ) % NZ * NX + (x + dx + NX) % NX) * 2 + side
            copy = pltpu.make_async_copy(
                part.at[pl.ds(p * ROWS, ROWS), :],
                factor.at[pl.ds(pl.multiple_of(base * ROWS, 32), ROWS), :],
                sems.at[count],
            )
            copy.start()
            copies[dz].append(copy)
            count += 1
    return copies


def stage_kernel(
    info, own_rows, early, early_swapped, sides, sides_swapped,
    factor, wide, token, sems, wide_sem,
):
    wide_copy = pltpu.make_async_copy(own_rows, wide.at[:BS], wide_sem)
    wide_copy.start()
    token[...] = jnp.zeros_like(token)
    sources = (
        (early, EARLY[:6], False),
        (sides, EARLY[6:], False),
        (early_swapped, EARLY[:6], True),
        (sides_swapped, EARLY[6:], True),
    )
    copies = fetch(info, factor, sems, sources)
    for copy in [wide_copy] + sum(copies.values(), []):
        copy.wait()


def stage(info, own_rows, early, early_swapped, sides, sides_swapped):
    smem = pl.BlockSpec(memory_space=pltpu.SMEM)
    vmem = pl.BlockSpec(memory_space=pltpu.VMEM)
    hbm = pl.BlockSpec(memory_space=pl.ANY)
    return pl.pallas_call(
        stage_kernel,
        out_shape=[
            pltpu.VMEM((SROWS, NC), jnp.bfloat16),
            pltpu.VMEM((2 * BS, SROWS), jnp.bfloat16),
            jax.ShapeDtypeStruct((8, BS), jnp.float32),
        ],
        in_specs=[smem, vmem] + [hbm] * 4,
        out_specs=[vmem] * 3,
        scratch_shapes=[
            pltpu.SemaphoreType.DMA((2 * len(EARLY),)),
            pltpu.SemaphoreType.DMA(()),
        ],
        compiler_params=pltpu.CompilerParams(vmem_limit_bytes=VMEM),
        name="stage",
    )(info, own_rows, early, early_swapped, sides, sides_swapped)


def product_kernel(
    info, _, __, ___, rows, late, late_swapped,
    factor, wide, own_out, other_out, turned, total, sems, wide_sem,
):
    wide_copy = pltpu.make_async_copy(rows, wide.at[BS:], wide_sem)
    wide_copy.start()
    sources = ((late, LATE, False), (late_swapped, LATE, True))
    copies = fetch(info, factor, sems, sources)
    wide_copy.wait()
    for s, (dz, waits) in enumerate(copies.items()):
        for copy in waits:
            copy.wait()
        start = pl.multiple_of((info[0] + dz + NZ) % NZ * ZROWS, BS)
        term = jnp.dot(
            wide[:, pl.ds(start, ZROWS)],
            factor[pl.ds(start, ZROWS), :],
            preferred_element_type=jnp.float32,
        )
        if s == 0:
            total[...] = term
        else:
            total[...] += term
    own = jnp.where(info[3] > 0, total[:BS], 0.0)
    other = jnp.where(info[4] > 0, total[BS:], 0.0)
    own_out[...] = -own
    other_out[...] = -other
    turned[:, :BS] = own.T.astype(jnp.bfloat16)
    turned[:, BS:] = other.T.astype(jnp.bfloat16)


def product(info, factor, wide, token, rows, late, late_swapped):
    smem = pl.BlockSpec(memory_space=pltpu.SMEM)
    vmem = pl.BlockSpec(memory_space=pltpu.VMEM)
    hbm = pl.BlockSpec(memory_space=pl.ANY)
    return pl.pallas_call(
        product_kernel,
        out_shape=[
            pltpu.VMEM((SROWS, NC), jnp.bfloat16),
            pltpu.VMEM((2 * BS, SROWS), jnp.bfloat16),
            jax.ShapeDtypeStruct((BS, NC), jnp.float32),
            jax.ShapeDtypeStruct((BS, NC), jnp.float32),
            jax.ShapeDtypeStruct((NC, 2 * BS), jnp.bfloat16),
        ],
        in_specs=[smem, vmem, vmem] + [hbm] * 4,
        out_specs=[vmem] * 5,
        input_output_aliases={1: 0, 2: 1},
        scratch_shapes=[
            pltpu.VMEM((2 * BS, NC), jnp.float32),
            pltpu.SemaphoreType.DMA((2 * len(LATE),)),
            pltpu.SemaphoreType.DMA(()),
        ],
        compiler_params=pltpu.CompilerParams(vmem_limit_bytes=VMEM),
        name="product",
    )(info, factor, wide, token, rows, late, late_swapped)


def partial_kernel(info, turned, factor, out, chosen):
    width = NC // NEAR
    for i in range(2 * NEAR):
        start = pl.multiple_of(info[8 + i] * BS, BS)
        chosen[i * BS : (i + 1) * BS, :] = factor[pl.ds(start, BS), :]
    left = jnp.concatenate(
        [turned[s * width : (s + 1) * width, :] for s in range(NEAR)], axis=1
    )
    total = jnp.dot(left, chosen[...], preferred_element_type=jnp.float32)
    tall = total.T
    for d in range(NBLK):
        first = tall[d * 16 : d * 16 + 8]
        second = tall[d * 16 + 8 : d * 16 + 16]
        out[d * 8 : (d + 1) * 8, :] = jnp.concatenate([first, second], axis=1)


def partial(info, turned, factor):
    smem = pl.BlockSpec(memory_space=pltpu.SMEM)
    vmem = pl.BlockSpec(memory_space=pltpu.VMEM)
    return pl.pallas_call(
        partial_kernel,
        out_shape=jax.ShapeDtypeStruct((NBLK * 8, BS), jnp.float32),
        in_specs=[smem, vmem, vmem],
        out_specs=vmem,
        scratch_shapes=[pltpu.VMEM((2 * NEAR * BS, NC), jnp.bfloat16)],
        compiler_params=pltpu.CompilerParams(vmem_limit_bytes=VMEM),
        name="partial",
    )(info, turned, factor)


def total_kernel(terms, diagonal, out):
    half = BS // 2
    for j in range(NEAR):
        tile = terms[j * 8 : (j + 1) * 8, :]
        for z in range(1, NZ):
            at = (z * NEAR + j) * 8
            tile = tile + terms[at : at + 8, :]
        columns = slice(j * half, (j + 1) * half)
        out[0:8, columns] = diagonal[0:8, columns] + tile[:, :half]
        out[8:16, columns] = diagonal[8:16, columns] + tile[:, half:]


def total(terms, diagonal):
    vmem = pl.BlockSpec(memory_space=pltpu.VMEM)
    return pl.pallas_call(
        total_kernel,
        out_shape=jax.ShapeDtypeStruct((NC // NBLK, NC), jnp.float32),
        in_specs=[vmem, vmem],
        out_specs=vmem,
        name="total",
    )(terms, diagonal)


def other_core(value):
    return ring(value, 0, 0, 1)


def onward(core, right, left):
    return ring(jnp.where(core == 0, right, left), 0, 1, 0, mirrored=True)


def body(parent_inverse, child_factor, child_diagonal, structure):
    blk = lax.axis_index("blk")
    front = lax.axis_index("front")
    half = front % 2
    zh, x, core = blk // NEAR, blk // 2 % NX, blk % 2
    mine = child_factor[0]
    lists = lax.dynamic_slice_in_dim(structure, front - half, 2, 0)
    lists = jnp.where(half == 0, lists, lists[::-1])
    listing = lists[0]
    near_at = zh * NEAR + jnp.arange(NEAR)
    blocks = jnp.stack(
        [half * (NPB // 2) + near_at, (1 - half) * (NPB // 2) + near_at], axis=1
    ).reshape(-1)
    position = jnp.sum((listing[None, :] < blocks[:, None]).astype(jnp.int32), axis=1)
    position = jnp.minimum(position, NS - 1)
    wanted = jnp.stack([half * (NPB // 2) + blk, (1 - half) * (NPB // 2) + blk])
    member = jnp.any(listing[None, :] == wanted[:, None], axis=1).astype(jnp.int32)
    info = jnp.concatenate(
        [jnp.stack([zh, x, core]), member, jnp.zeros((3,), jnp.int32), position]
    )

    near = [mine] + [ring(mine, 0, dx, 0) for dx in (1, -1)]
    up = ring(mine, 1, 0, 0)
    down = ring(mine, -1, 0, 0)
    near, lists, info, up, down = lax.optimization_barrier((near, lists, info, up, down))

    across = ring(jnp.where(core == 0, up, down), 1, 0, 0, mirrored=True)
    own_rows, *sends = pick(lists, parent_inverse[0])
    own_rows, sends, across = lax.optimization_barrier((own_rows, sends, across))
    trio = jnp.concatenate([up, down, across], axis=0)
    right = ring(trio, 0, 1, 0)
    left = ring(trio, 0, -1, 0)
    trio, right, left = lax.optimization_barrier((trio, right, left))
    early = jnp.concatenate([*near, trio], axis=0)
    early_swapped = other_core(early)
    sides = jnp.concatenate([right, left], axis=0)
    sides_swapped = other_core(sides)
    late = onward(
        core,
        jnp.concatenate([near[1], right], axis=0),
        jnp.concatenate([near[2], left], axis=0),
    )
    other_rows = partner(sends[0])
    factor, wide, token = stage(
        info, own_rows, early, early_swapped, sides, sides_swapped
    )
    late, other_rows, token = lax.optimization_barrier((late, other_rows, token))
    late_swapped = other_core(late)
    factor, _, own_out, other_out, turned = product(
        info, factor, wide, token, other_rows, late, late_swapped
    )
    second = partner(other_out)
    groups = [[z * NEAR + i for i in range(NEAR)] for z in range(NZ)]
    turned = lax.all_to_all(
        turned, "blk", 0, 0, axis_index_groups=groups, tiled=True
    )
    terms = lax.all_to_all(partial(info, turned, factor), "blk", 0, 0, tiled=True)
    inverse = total(terms, child_diagonal[0])
    placed = jnp.stack([own_out, second], axis=1)
    return placed[None], inverse[None]


def solution(mesh):
    in_specs = (P("front", "blk", None), P("front", "blk", None), P("front", "blk", None), P())
    out_specs = (P("front", "blk", None, None), P("front", "blk", None))
    return jax.shard_map(body, mesh=mesh, in_specs=in_specs, out_specs=out_specs, check_vma=False)
```

time: 173 us -> 133 us (0.77)
  starting transfers between devices: 102 us -> 72.7 us
  waiting for transfers between devices: 31.2 us -> 24.6 us
  local copies, waits for them, and re-layouts: 9.78 us -> 4.59 us
  other arithmetic: 4.27 us -> 1.44 us
    ppermute x15 -> x11, starting transfers between devices: 86.7 us -> 53.4 us  [ring(): return lax.ppermute(value, 'blk', pairs)]
    ppermute x2, starting transfers between devices: 3.83 us -> 12 us  [partner(): return lax.ppermute(value, 'front', pairs)]
    ppermute x15 -> x11, waiting for transfers between devices: 18.9 us -> 11.2 us  [ring(): return lax.ppermute(value, 'blk', pairs)]
    ppermute x2, waiting for transfers between devices: 8.56 us -> 13.3 us  [partner(): return lax.ppermute(value, 'front', pairs)]
    all_to_all x1, starting transfers between devices: 11.5 us -> 7.33 us  [body(): lax.all_to_all(partial(info, turned, factor), 'blk', 0, 0, tiled=True)]
    all_to_all x1, waiting for transfers between devices: 3.72 us -> 0.1 us  [body(): lax.all_to_all(partial(info, turned, factor), 'blk', 0, 0, tiled=True)]
    unnamed x17 -> x12, local copies, waits for them, and re-layouts: 7.14 us -> 3.53 us
    select_n x4 -> x2, other arithmetic: 2.64 us -> 0.89 us  [the longest x1 0.7 us: body(): lists = jnp.where(half == 0, lists, lists[::-1])]
  transfers between devices with their start and end apart: 18 -> 14, of which waited for: 5 -> 9; matrix products, arithmetic and copies ran while one was open for 5% -> 3% of each run, Pallas kernels for 1% -> 6%
where the time goes in v2:
time: 133 us; the launch traced here: 130 us
  starting transfers between devices  72.7 us (55%)
  waiting for transfers between devices  24.6 us (18%)
  Pallas kernels  15.2 us (11%)
  blocking collectives  10.9 us (8%)
  local copies, waits for them, and re-layouts  4.59 us (3%)
  other arithmetic  1.44 us (1%)
    ppermute x11, starting transfers between devices, ring(): return lax.ppermute(value, 'blk', pairs)  53.4 us
    ppermute x2, waiting for transfers between devices, partner(): return lax.ppermute(value, 'front', pairs)  13.3 us
    ppermute x2, starting transfers between devices, partner(): return lax.ppermute(value, 'front', pairs)  12 us
    ppermute x11, waiting for transfers between devices, ring(): return lax.ppermute(value, 'blk', pairs)  11.2 us
    all_to_all x1, blocking collectives, body(): lax.all_to_all(turned, 'blk', 0, 0, axis_index_groups=groups, tiled=True)  10.9 us
    all_to_all x1, starting transfers between devices, body(): lax.all_to_all(partial(info, turned, factor), 'blk', 0, 0, tiled=True)  7.33 us
    pallas_call x1, Pallas kernels, stage(): pl.pallas_call(stage_kernel, out_shape=[pltpu.VMEM((SROWS, NC), jnp.bfloa...  6.31 us
    pallas_call x1, Pallas kernels, product(): pl.pallas_call(product_kernel, out_shape=[pltpu.VMEM((SROWS, NC), jnp.bfl...  4.22 us
  transfers between devices with their start and end apart: 14, of which 9 were waited for; matrix products, arithmetic and copies ran while one was open for 3% of the time, Pallas kernels for 6%

profile of v2, /device:TPU:1, one launch (start us, length us, event | category | flops | bytes accessed | tf_op | source)
XLA Modules:
  0.0 130.5 jit_solution(13713854957158743943)
XLA Ops:
  0.6 13.3 %collective-permute-start.3 = (bf16[160,512]{1,0:T(8,128)(2,1)}, bf16[160,512]{1,0:T(8,128)(2,1)S(1)}, u32[]{:S(2)}, u32[]{:S(2)}) collective-permute-start(bf16[160,512]{1,0:T(8,128)(2,1)} %bitcast.25), channel_id=1, source_target_pairs={{0,24},{1,25},{2,26},{3,27},{4,28},{5,29},{6,30},{7,31},{8,0},{9,1... | collective-permute-start | bytes 491528 | tf_op jit(solution)/shard_map/ppermute | solution.py:29
  13.9 1.9 %collective-permute-start.2 = (bf16[160,512]{1,0:T(8,128)(2,1)}, bf16[160,512]{1,0:T(8,128)(2,1)S(1)}, u32[]{:S(2)}, u32[]{:S(2)}) collective-permute-start(bf16[160,512]{1,0:T(8,128)(2,1)} %bitcast.26), channel_id=1, source_target_pairs={{0,8},{1,9},{2,10},{3,11},{4,12},{5,13},{6,14},{7,15},{8,16},{9,17... | collective-permute-start | bytes 491528 | tf_op jit(solution)/shard_map/ppermute | solution.py:29
  15.9 4.4 %collective-permute-start.1 = (bf16[160,512]{1,0:T(8,128)(2,1)}, bf16[160,512]{1,0:T(8,128)(2,1)S(1)}, u32[]{:S(2)}, u32[]{:S(2)}) collective-permute-start(bf16[160,512]{1,0:T(8,128)(2,1)} %bitcast.27), channel_id=1, source_target_pairs={{0,6},{1,7},{2,0},{3,1},{4,2},{5,3},{6,4},{7,5},{8,14},{9,15},{10,... | collective-permute-start | bytes 491528 | tf_op jit(solution)/shard_map/ppermute | solution.py:29
  20.3 1.9 %collective-permute-start = (bf16[160,512]{1,0:T(8,128)(2,1)}, bf16[160,512]{1,0:T(8,128)(2,1)S(1)}, u32[]{:S(2)}, u32[]{:S(2)}) collective-permute-start(bf16[160,512]{1,0:T(8,128)(2,1)} %bitcast.28), channel_id=1, source_target_pairs={{0,2},{1,3},{2,4},{3,5},{4,6},{5,7},{6,0},{7,1},{8,10},{9,11},{10,... | collective-permute-start | bytes 491528 | tf_op jit(solution)/shard_map/ppermute | solution.py:29
  22.3 0.7 constant_dynamic-slice_fusion
  23.0 0.7 broadcast_select_fusion.1.lists
  24.5 3.7 %collective-permute-done.3 = bf16[160,512]{1,0:T(8,128)(2,1)S(1)} collective-permute-done((bf16[160,512]{1,0:T(8,128)(2,1)}, bf16[160,512]{1,0:T(8,128)(2,1)S(1)}, u32[]{:S(2)}, u32[]{:S(2)}) %collective-permute-start.3) | collective-permute-done | bytes 163872 | tf_op jit(solution)/shard_map/ppermute | solution.py:29
  28.2 8.2 %collective-permute-start.4 = (bf16[160,512]{1,0:T(8,128)(2,1)S(1)}, bf16[160,512]{1,0:T(8,128)(2,1)S(1)}, u32[]{:S(2)}, u32[]{:S(2)}) collective-permute-start(bf16[160,512]{1,0:T(8,128)(2,1)S(1)} %get-tuple-element.61), channel_id=1, source_target_pairs={{0,8},{1,25},{2,10},{3,27},{4,12},{5,29},{6,14},{7,31},{8,16},{9,1... | collective-permute-start | bytes 491528 | tf_op jit(solution)/shard_map/ppermute | solution.py:29
  36.4 1.6 %copy-done = bf16[1,128,8192]{2,1,0:T(8,128)(2,1)S(1)} copy-done((bf16[1,128,8192]{2,1,0:T(8,128)(2,1)S(1)}, bf16[1,128,8192]{2,1,0:T(8,128)(2,1)}, u32[]{:S(2)}) %copy-start) | copy-done | bytes 2097176
  38.0 1.2 pick.1
  39.3 1.2 collective-permute-done.4
  40.4 4.4 %collective-permute-start.6 = (bf16[480,512]{1,0:T(8,128)(2,1)S(1)}, bf16[480,512]{1,0:T(8,128)(2,1)S(1)}, u32[]{:S(2)}, u32[]{:S(2)}) collective-permute-start(bf16[480,512]{1,0:T(8,128)(2,1)S(1)} %constant_dynamic-update-slice_fusion), channel_id=1, source_target_pairs={{0,6},{1,7},{2,0},{3,1},{4,2},{5,3},{6,4},{7,5},{8,14},{9,15},{10,... | collective-permute-start | bytes 1474568 | tf_op jit(solution)/shard_map/ppermute | solution.py:29
  44.8 1.9 %collective-permute-start.5 = (bf16[480,512]{1,0:T(8,128)(2,1)S(1)}, bf16[480,512]{1,0:T(8,128)(2,1)S(1)}, u32[]{:S(2)}, u32[]{:S(2)}) collective-permute-start(bf16[480,512]{1,0:T(8,128)(2,1)S(1)} %constant_dynamic-update-slice_fusion), channel_id=1, source_target_pairs={{0,2},{1,3},{2,4},{3,5},{4,6},{5,7},{6,0},{7,1},{8,10},{9,11},{10,... | collective-permute-start | bytes 1474568 | tf_op jit(solution)/shard_map/ppermute | solution.py:29
  46.8 7.5 %collective-permute-start.10 = (bf16[128,5120]{1,0:T(8,128)(2,1)S(1)}, bf16[128,5120]{1,0:T(8,128)(2,1)S(1)}, u32[]{:S(2)}, u32[]{:S(2)}) collective-permute-start(bf16[128,5120]{1,0:T(8,128)(2,1)S(1)} %get-tuple-element.43), channel_id=1, source_target_pairs={{0,32},{32,0},{64,96},{96,64},{128,160},{160,128},{192,224},{224,1... | collective-permute-start | bytes 3932168 | tf_op jit(solution)/shard_map/ppermute | solution.py:34
  54.4 1.2 collective-permute-done.5
  55.7 8.4 %collective-permute-start.8 = (bf16[960,512]{1,0:T(8,128)(2,1)S(1)}, bf16[960,512]{1,0:T(8,128)(2,1)S(1)}, u32[]{:S(2)}, u32[]{:S(2)}) collective-permute-start(bf16[960,512]{1,0:T(8,128)(2,1)S(1)} %constant_dynamic-update-slice_fusion.7.sides), channel_id=1, source_target_pairs={{0,1},{1,0},{2,3},{3,2},{4,5},{5,4},{6,7},{7,6},{8,9},{9,8},{10,11... | collective-permute-start | bytes 2949128 | tf_op jit(solution)/shard_map/ppermute | solution.py:29
  64.1 1.9 %collective-permute-start.7 = (bf16[960,512]{1,0:T(8,128)(2,1)S(1)}, bf16[960,512]{1,0:T(8,128)(2,1)S(1)}, u32[]{:S(2)}, u32[]{:S(2)}) collective-permute-start(bf16[960,512]{1,0:T(8,128)(2,1)S(1)} %constant_dynamic-update-slice_fusion.3.early), channel_id=1, source_target_pairs={{0,1},{1,0},{2,3},{3,2},{4,5},{5,4},{6,7},{7,6},{8,9},{9,8},{10,11... | collective-permute-start | bytes 2949128 | tf_op jit(solution)/shard_map/ppermute | solution.py:29
  66.2 1.9 %collective-permute-start.9 = (bf16[640,512]{1,0:T(8,128)(2,1)S(1)}, bf16[640,512]{1,0:T(8,128)(2,1)S(1)}, u32[]{:S(2)}, u32[]{:S(2)}) collective-permute-start(bf16[640,512]{1,0:T(8,128)(2,1)S(1)} %maximum_select_fusion), channel_id=1, source_target_pairs={{0,2},{1,7},{2,4},{3,1},{4,6},{5,3},{6,0},{7,5},{8,10},{9,15},{10,... | collective-permute-start | bytes 1966088 | tf_op jit(solution)/shard_map/ppermute | solution.py:29
  68.6 6.3 %stage.1 = (bf16[5120,512]{1,0:T(8,128)(2,1)S(1)}, bf16[256,5120]{1,0:T(8,128)(2,1)S(1)}, f32[8,128]{1,0:T(8,128)S(1)}) custom-call(s32[24]{0:T(128)S(1)} %concatenate.18.info, bf16[128,5120]{1,0:T(8,128)(2,1)S(1)} %get-tuple-element.33.own_rows, bf16[960,512]{1,0:T(8,128)(2,1)S(1)} %constant_dynamic-update-slice_fusion.3.early, ...), custom_call_target="tpu_custom_call" | custom-call | tf_op jit(solution)/shard_map/stage/pallas_call | solution.py:113
  74.9 3.0 %collective-permute-done.9.late = bf16[640,512]{1,0:T(8,128)(2,1)S(1)} collective-permute-done((bf16[640,512]{1,0:T(8,128)(2,1)S(1)}, bf16[640,512]{1,0:T(8,128)(2,1)S(1)}, u32[]{:S(2)}, u32[]{:S(2)}) %collective-permute-start.9) | collective-permute-done | bytes 655392 | tf_op jit(solution)/shard_map/ppermute | solution.py:29
  77.9 3.0 %collective-permute-done.10.rows = bf16[128,5120]{1,0:T(8,128)(2,1)S(1)} collective-permute-done((bf16[128,5120]{1,0:T(8,128)(2,1)S(1)}, bf16[128,5120]{1,0:T(8,128)(2,1)S(1)}, u32[]{:S(2)}, u32[]{:S(2)}) %collective-permute-start.10) | collective-permute-done | bytes 1310752 | tf_op jit(solution)/shard_map/ppermute | solution.py:34
  80.8 5.2 %collective-permute-start.11 = (bf16[640,512]{1,0:T(8,128)(2,1)S(1)}, bf16[640,512]{1,0:T(8,128)(2,1)S(1)}, u32[]{:S(2)}, u32[]{:S(2)}) collective-permute-start(bf16[640,512]{1,0:T(8,128)(2,1)S(1)} %collective-permute-done.9.late), channel_id=1, source_target_pairs={{0,1},{1,0},{2,3},{3,2},{4,5},{5,4},{6,7},{7,6},{8,9},{9,8},{10,11... | collective-permute-start | bytes 1966088 | tf_op jit(solution)/shard_map/ppermute | solution.py:29
  86.0 1.7 %collective-permute-done.11.late_swapped = bf16[640,512]{1,0:T(8,128)(2,1)S(1)} collective-permute-done((bf16[640,512]{1,0:T(8,128)(2,1)S(1)}, bf16[640,512]{1,0:T(8,128)(2,1)S(1)}, u32[]{:S(2)}, u32[]{:S(2)}) %collective-permute-start.11) | collective-permute-done | bytes 655392 | tf_op jit(solution)/shard_map/ppermute | solution.py:29
  87.7 4.2 %product.1 = (bf16[5120,512]{1,0:T(8,128)(2,1)S(1)}, bf16[256,5120]{1,0:T(8,128)(2,1)S(1)}, f32[128,512]{1,0:T(8,128)S(1)}, f32[128,512]{1,0:T(8,128)S(1)}, bf16[512,256]{1,0:T(8,128)(2,1)S(1)}) custom-call(s32[24]{0:T(128)S(1)} %concatenate.18.info, bf16[5120,512]{1,0:T(8,128)(2,1)S(1)} %get-tuple-element.41._, ...), custom_call_target="tpu_custom_call", output_to_operand_aliasing={{0}: (1, {}), {1}: (2, {})} | custom-call | tf_op jit(solution)/shard_map/product/pallas_call | solution.py:165
  91.9 10.9 %all_to_all.22 = bf16[8,64,256]{2,1,0:T(8,128)(2,1)S(1)} all-to-all(bf16[8,64,256]{2,1,0:T(8,128)(2,1)S(1)} %bitcast.21), channel_id=1, replica_groups={{0,1,2,3,4,5,6,7},{8,9,10,11,12,13,14,15},{16,17,18,19,20,21,22,23},{24..., dimensions={0} | all-to-all | bytes 524288 | tf_op jit(solution)/shard_map/all_to_all | solution.py:301
  102.8 1.9 %partial.1 = f32[256,128]{1,0:T(8,128)} custom-call(s32[24]{0:T(128)S(1)} %concatenate.18.info, bf16[512,256]{1,0:T(8,128)(2,1)S(1)} %bitcast.20, bf16[5120,512]{1,0:T(8,128)(2,1)S(1)} %get-tuple-element.51.factor), custom_call_target="tpu_custom_call" | custom-call | tf_op jit(solution)/shard_map/partial/pallas_call | solution.py:206
  104.7 7.3 %all-to-all-start.1 = ((f32[32,8,128]{2,1,0:T(8,128)}), f32[32,8,128]{2,1,0:T(8,128)S(1)}, u32[]{:S(2)}, u32[]{:S(2)}) async-start(f32[32,8,128]{2,1,0:T(8,128)} %bitcast.13), calls=%async_computation.1 | async-start | bytes 262144 | tf_op jit(solution)/shard_map/all_to_all | solution.py:304
  112.0 4.4 %collective-permute-start.12 = (f32[128,512]{1,0:T(8,128)S(1)}, f32[128,512]{1,0:T(8,128)S(1)}, u32[]{:S(2)}, u32[]{:S(2)}) collective-permute-start(f32[128,512]{1,0:T(8,128)S(1)} %get-tuple-element.49), channel_id=1, source_target_pairs={{0,32},{32,0},{64,96},{96,64},{128,160},{160,128},{192,224},{224,1... | collective-permute-start | bytes 786440 | tf_op jit(solution)/shard_map/ppermute | solution.py:34
  116.5 10.4 %collective-permute-done.12 = f32[128,512]{1,0:T(8,128)S(1)} collective-permute-done((f32[128,512]{1,0:T(8,128)S(1)}, f32[128,512]{1,0:T(8,128)S(1)}, u32[]{:S(2)}, u32[]{:S(2)}) %collective-permute-start.12) | collective-permute-done | bytes 262176 | tf_op jit(solution)/shard_map/ppermute | solution.py:34
  126.9 1.2 copy.13
  128.2 0.7 copy-done.1
  128.9 1.6 %total.1 = f32[16,512]{1,0:T(8,128)} custom-call(f32[256,128]{1,0:T(8,128)} %bitcast.23, f32[16,512]{1,0:T(8,128)} %bitcast.30), custom_call_target="tpu_custom_call" | custom-call | tf_op jit(solution)/shard_map/total/pallas_call | solution.py:231
  (35 shorter events, 1.7 us)
Async XLA Ops:
  0.6 27.5 %collective-permute-start.3 = (bf16[160,512]{1,0:T(8,128)(2,1)}, bf16[160,512]{1,0:T(8,128)(2,1)S(1)}, u32[]{:S(2)}, u32[]{:S(2)}) collective-permute-start(bf16[160,512]{1,0:T(8,128)(2,1)} %bitcast.25), channel_id=1, source_target_pairs={{0,24},{1,25},{2,26},{3,27},{4,28},{5,29},{6,30},{7,31},{8,0},{9,1... | collective-permute-start | bytes 491528 | tf_op jit(solution)/shard_map/ppermute | solution.py:29
  13.9 14.2 %collective-permute-start.2 = (bf16[160,512]{1,0:T(8,128)(2,1)}, bf16[160,512]{1,0:T(8,128)(2,1)S(1)}, u32[]{:S(2)}, u32[]{:S(2)}) collective-permute-start(bf16[160,512]{1,0:T(8,128)(2,1)} %bitcast.26), channel_id=1, source_target_pairs={{0,8},{1,9},{2,10},{3,11},{4,12},{5,13},{6,14},{7,15},{8,16},{9,17... | collective-permute-start | bytes 491528 | tf_op jit(solution)/shard_map/ppermute | solution.py:29
  15.9 12.3 %collective-permute-start.1 = (bf16[160,512]{1,0:T(8,128)(2,1)}, bf16[160,512]{1,0:T(8,128)(2,1)S(1)}, u32[]{:S(2)}, u32[]{:S(2)}) collective-permute-start(bf16[160,512]{1,0:T(8,128)(2,1)} %bitcast.27), channel_id=1, source_target_pairs={{0,6},{1,7},{2,0},{3,1},{4,2},{5,3},{6,4},{7,5},{8,14},{9,15},{10,... | collective-permute-start | bytes 491528 | tf_op jit(solution)/shard_map/ppermute | solution.py:29
  20.3 7.9 %collective-permute-start = (bf16[160,512]{1,0:T(8,128)(2,1)}, bf16[160,512]{1,0:T(8,128)(2,1)S(1)}, u32[]{:S(2)}, u32[]{:S(2)}) collective-permute-start(bf16[160,512]{1,0:T(8,128)(2,1)} %bitcast.28), channel_id=1, source_target_pairs={{0,2},{1,3},{2,4},{3,5},{4,6},{5,7},{6,0},{7,1},{8,10},{9,11},{10,... | collective-permute-start | bytes 491528 | tf_op jit(solution)/shard_map/ppermute | solution.py:29
  28.2 18.6 %copy-start.2 = (bf16[1,160,512]{2,1,0:T(8,128)(2,1)S(1)}, bf16[1,160,512]{2,1,0:T(8,128)(2,1)}, u32[]{:S(2)}) copy-start(bf16[1,160,512]{2,1,0:T(8,128)(2,1)} %param.5) | copy-start | bytes 491524
  28.2 12.2 %collective-permute-start.4 = (bf16[160,512]{1,0:T(8,128)(2,1)S(1)}, bf16[160,512]{1,0:T(8,128)(2,1)S(1)}, u32[]{:S(2)}, u32[]{:S(2)}) collective-permute-start(bf16[160,512]{1,0:T(8,128)(2,1)S(1)} %get-tuple-element.61), channel_id=1, source_target_pairs={{0,8},{1,25},{2,10},{3,27},{4,12},{5,29},{6,14},{7,31},{8,16},{9,1... | collective-permute-start | bytes 491528 | tf_op jit(solution)/shard_map/ppermute | solution.py:29
  36.4 1.6 %copy-start = (bf16[1,128,8192]{2,1,0:T(8,128)(2,1)S(1)}, bf16[1,128,8192]{2,1,0:T(8,128)(2,1)}, u32[]{:S(2)}) copy-start(bf16[1,128,8192]{2,1,0:T(8,128)(2,1)} %param.4) | copy-start | bytes 6291460
  40.4 13.9 %collective-permute-start.6 = (bf16[480,512]{1,0:T(8,128)(2,1)S(1)}, bf16[480,512]{1,0:T(8,128)(2,1)S(1)}, u32[]{:S(2)}, u32[]{:S(2)}) collective-permute-start(bf16[480,512]{1,0:T(8,128)(2,1)S(1)} %constant_dynamic-update-slice_fusion), channel_id=1, source_target_pairs={{0,6},{1,7},{2,0},{3,1},{4,2},{5,3},{6,4},{7,5},{8,14},{9,15},{10,... | collective-permute-start | bytes 1474568 | tf_op jit(solution)/shard_map/ppermute | solution.py:29
  44.8 10.8 %collective-permute-start.5 = (bf16[480,512]{1,0:T(8,128)(2,1)S(1)}, bf16[480,512]{1,0:T(8,128)(2,1)S(1)}, u32[]{:S(2)}, u32[]{:S(2)}) collective-permute-start(bf16[480,512]{1,0:T(8,128)(2,1)S(1)} %constant_dynamic-update-slice_fusion), channel_id=1, source_target_pairs={{0,2},{1,3},{2,4},{3,5},{4,6},{5,7},{6,0},{7,1},{8,10},{9,11},{10,... | collective-permute-start | bytes 1474568 | tf_op jit(solution)/shard_map/ppermute | solution.py:29
  46.8 34.0 %collective-permute-start.10 = (bf16[128,5120]{1,0:T(8,128)(2,1)S(1)}, bf16[128,5120]{1,0:T(8,128)(2,1)S(1)}, u32[]{:S(2)}, u32[]{:S(2)}) collective-permute-start(bf16[128,5120]{1,0:T(8,128)(2,1)S(1)} %get-tuple-element.43), channel_id=1, source_target_pairs={{0,32},{32,0},{64,96},{96,64},{128,160},{160,128},{192,224},{224,1... | collective-permute-start | bytes 3932168 | tf_op jit(solution)/shard_map/ppermute | solution.py:34
  55.7 12.5 %collective-permute-start.8 = (bf16[960,512]{1,0:T(8,128)(2,1)S(1)}, bf16[960,512]{1,0:T(8,128)(2,1)S(1)}, u32[]{:S(2)}, u32[]{:S(2)}) collective-permute-start(bf16[960,512]{1,0:T(8,128)(2,1)S(1)} %constant_dynamic-update-slice_fusion.7.sides), channel_id=1, source_target_pairs={{0,1},{1,0},{2,3},{3,2},{4,5},{5,4},{6,7},{7,6},{8,9},{9,8},{10,11... | collective-permute-start | bytes 2949128 | tf_op jit(solution)/shard_map/ppermute | solution.py:29
  64.1 4.5 %collective-permute-start.7 = (bf16[960,512]{1,0:T(8,128)(2,1)S(1)}, bf16[960,512]{1,0:T(8,128)(2,1)S(1)}, u32[]{:S(2)}, u32[]{:S(2)}) collective-permute-start(bf16[960,512]{1,0:T(8,128)(2,1)S(1)} %constant_dynamic-update-slice_fusion.3.early), channel_id=1, source_target_pairs={{0,1},{1,0},{2,3},{3,2},{4,5},{5,4},{6,7},{7,6},{8,9},{9,8},{10,11... | collective-permute-start | bytes 2949128 | tf_op jit(solution)/shard_map/ppermute | solution.py:29
  66.2 11.6 %collective-permute-start.9 = (bf16[640,512]{1,0:T(8,128)(2,1)S(1)}, bf16[640,512]{1,0:T(8,128)(2,1)S(1)}, u32[]{:S(2)}, u32[]{:S(2)}) collective-permute-start(bf16[640,512]{1,0:T(8,128)(2,1)S(1)} %maximum_select_fusion), channel_id=1, source_target_pairs={{0,2},{1,7},{2,4},{3,1},{4,6},{5,3},{6,0},{7,5},{8,10},{9,15},{10,... | collective-permute-start | bytes 1966088 | tf_op jit(solution)/shard_map/ppermute | solution.py:29
  80.8 6.9 %collective-permute-start.11 = (bf16[640,512]{1,0:T(8,128)(2,1)S(1)}, bf16[640,512]{1,0:T(8,128)(2,1)S(1)}, u32[]{:S(2)}, u32[]{:S(2)}) collective-permute-start(bf16[640,512]{1,0:T(8,128)(2,1)S(1)} %collective-permute-done.9.late), channel_id=1, source_target_pairs={{0,1},{1,0},{2,3},{3,2},{4,5},{5,4},{6,7},{7,6},{8,9},{9,8},{10,11... | collective-permute-start | bytes 1966088 | tf_op jit(solution)/shard_map/ppermute | solution.py:29
  104.7 23.5 %all-to-all-start.1 = ((f32[32,8,128]{2,1,0:T(8,128)}), f32[32,8,128]{2,1,0:T(8,128)S(1)}, u32[]{:S(2)}, u32[]{:S(2)}) async-start(f32[32,8,128]{2,1,0:T(8,128)} %bitcast.13), calls=%async_computation.1 | async-start | bytes 262144 | tf_op jit(solution)/shard_map/all_to_all | solution.py:304
  112.0 14.8 %collective-permute-start.12 = (f32[128,512]{1,0:T(8,128)S(1)}, f32[128,512]{1,0:T(8,128)S(1)}, u32[]{:S(2)}, u32[]{:S(2)}) collective-permute-start(f32[128,512]{1,0:T(8,128)S(1)} %get-tuple-element.49), channel_id=1, source_target_pairs={{0,32},{32,0},{64,96},{96,64},{128,160},{160,128},{192,224},{224,1... | collective-permute-start | bytes 786440 | tf_op jit(solution)/shard_map/ppermute | solution.py:34
  128.2 0.7 copy-start.1

commit v3 on v2

--- a/solution.py
+++ b/solution.py
@@ -214,25 +214,41 @@
     )(info, turned, factor)
 
 
-def total_kernel(terms, diagonal, out):
+def total_kernel(terms, diagonal, out, held, base, sems):
+    copies = [pltpu.make_async_copy(diagonal, base, sems.at[0])]
+    for z in range(NZ):
+        rows = pl.ds(z * NEAR * 8, NEAR * 8)
+        copies.append(
+            pltpu.make_async_copy(terms.at[rows], held.at[rows], sems.at[z + 1])
+        )
+    for copy in copies:
+        copy.start()
+    for copy in copies:
+        copy.wait()
     half = BS // 2
     for j in range(NEAR):
-        tile = terms[j * 8 : (j + 1) * 8, :]
+        tile = held[j * 8 : (j + 1) * 8, :]
         for z in range(1, NZ):
             at = (z * NEAR + j) * 8
-            tile = tile + terms[at : at + 8, :]
+            tile = tile + held[at : at + 8, :]
         columns = slice(j * half, (j + 1) * half)
-        out[0:8, columns] = diagonal[0:8, columns] + tile[:, :half]
-        out[8:16, columns] = diagonal[8:16, columns] + tile[:, half:]
+        out[0:8, columns] = base[0:8, columns] + tile[:, :half]
+        out[8:16, columns] = base[8:16, columns] + tile[:, half:]
 
 
 def total(terms, diagonal):
-    vmem = pl.BlockSpec(memory_space=pltpu.VMEM)
+    hbm = pl.BlockSpec(memory_space=pl.ANY)
     return pl.pallas_call(
         total_kernel,
         out_shape=jax.ShapeDtypeStruct((NC // NBLK, NC), jnp.float32),
-        in_specs=[vmem, vmem],
-        out_specs=vmem,
+        in_specs=[hbm, hbm],
+        out_specs=pl.BlockSpec(memory_space=pltpu.VMEM),
+        scratch_shapes=[
+            pltpu.VMEM((NBLK * 8, BS), jnp.float32),
+            pltpu.VMEM((NC // NBLK, NC), jnp.float32),
+            pltpu.SemaphoreType.DMA((1 + NZ,)),
+        ],
+        compiler_params=pltpu.CompilerParams(vmem_limit_bytes=60 * 1024 * 1024),
         name="total",
     )(terms, diagonal)
 

time: 133 us -> 133 us (level)
  no operation moved by 1% of the time
where the time goes in v3:
time: 133 us; the launch traced here: 130 us
  starting transfers between devices  72.7 us (55%)
  waiting for transfers between devices  24.6 us (18%)
  Pallas kernels  15.2 us (11%)
  blocking collectives  10.9 us (8%)
  local copies, waits for them, and re-layouts  4.59 us (3%)
  other arithmetic  1.44 us (1%)
    ppermute x11, starting transfers between devices, ring(): return lax.ppermute(value, 'blk', pairs)  53.4 us
    ppermute x2, waiting for transfers between devices, partner(): return lax.ppermute(value, 'front', pairs)  13.3 us
    ppermute x2, starting transfers between devices, partner(): return lax.ppermute(value, 'front', pairs)  12 us
    ppermute x11, waiting for transfers between devices, ring(): return lax.ppermute(value, 'blk', pairs)  11.2 us
    all_to_all x1, blocking collectives, body(): lax.all_to_all(turned, 'blk', 0, 0, axis_index_groups=groups, tiled=True)  10.9 us
    all_to_all x1, starting transfers between devices, body(): lax.all_to_all(partial(info, turned, factor), 'blk', 0, 0, tiled=True)  7.33 us
    pallas_call x1, Pallas kernels, stage(): pl.pallas_call(stage_kernel, out_shape=[pltpu.VMEM((SROWS, NC), jnp.bfloa...  6.31 us
    pallas_call x1, Pallas kernels, product(): pl.pallas_call(product_kernel, out_shape=[pltpu.VMEM((SROWS, NC), jnp.bfl...  4.22 us
  transfers between devices with their start and end apart: 14, of which 9 were waited for; matrix products, arithmetic and copies ran while one was open for 3% of the time, Pallas kernels for 6%

profile of v3, /device:TPU:1, one launch (start us, length us, event | category | flops | bytes accessed | tf_op | source)
XLA Modules:
  0.0 130.4 jit_solution(18248573756070672848)
XLA Ops:
  0.6 13.3 %collective-permute-start.3 = (bf16[160,512]{1,0:T(8,128)(2,1)}, bf16[160,512]{1,0:T(8,128)(2,1)S(1)}, u32[]{:S(2)}, u32[]{:S(2)}) collective-permute-start(bf16[160,512]{1,0:T(8,128)(2,1)} %bitcast.25), channel_id=1, source_target_pairs={{0,24},{1,25},{2,26},{3,27},{4,28},{5,29},{6,30},{7,31},{8,0},{9,1... | collective-permute-start | bytes 491528 | tf_op jit(solution)/shard_map/ppermute | solution.py:29
  13.9 1.9 %collective-permute-start.2 = (bf16[160,512]{1,0:T(8,128)(2,1)}, bf16[160,512]{1,0:T(8,128)(2,1)S(1)}, u32[]{:S(2)}, u32[]{:S(2)}) collective-permute-start(bf16[160,512]{1,0:T(8,128)(2,1)} %bitcast.26), channel_id=1, source_target_pairs={{0,8},{1,9},{2,10},{3,11},{4,12},{5,13},{6,14},{7,15},{8,16},{9,17... | collective-permute-start | bytes 491528 | tf_op jit(solution)/shard_map/ppermute | solution.py:29
  15.9 4.4 %collective-permute-start.1 = (bf16[160,512]{1,0:T(8,128)(2,1)}, bf16[160,512]{1,0:T(8,128)(2,1)S(1)}, u32[]{:S(2)}, u32[]{:S(2)}) collective-permute-start(bf16[160,512]{1,0:T(8,128)(2,1)} %bitcast.27), channel_id=1, source_target_pairs={{0,6},{1,7},{2,0},{3,1},{4,2},{5,3},{6,4},{7,5},{8,14},{9,15},{10,... | collective-permute-start | bytes 491528 | tf_op jit(solution)/shard_map/ppermute | solution.py:29
  20.3 1.9 %collective-permute-start = (bf16[160,512]{1,0:T(8,128)(2,1)}, bf16[160,512]{1,0:T(8,128)(2,1)S(1)}, u32[]{:S(2)}, u32[]{:S(2)}) collective-permute-start(bf16[160,512]{1,0:T(8,128)(2,1)} %bitcast.28), channel_id=1, source_target_pairs={{0,2},{1,3},{2,4},{3,5},{4,6},{5,7},{6,0},{7,1},{8,10},{9,11},{10,... | collective-permute-start | bytes 491528 | tf_op jit(solution)/shard_map/ppermute | solution.py:29
  22.3 0.7 constant_dynamic-slice_fusion
  23.0 0.7 broadcast_select_fusion.1.lists
  24.5 3.7 %collective-permute-done.3 = bf16[160,512]{1,0:T(8,128)(2,1)S(1)} collective-permute-done((bf16[160,512]{1,0:T(8,128)(2,1)}, bf16[160,512]{1,0:T(8,128)(2,1)S(1)}, u32[]{:S(2)}, u32[]{:S(2)}) %collective-permute-start.3) | collective-permute-done | bytes 163872 | tf_op jit(solution)/shard_map/ppermute | solution.py:29
  28.2 8.2 %collective-permute-start.4 = (bf16[160,512]{1,0:T(8,128)(2,1)S(1)}, bf16[160,512]{1,0:T(8,128)(2,1)S(1)}, u32[]{:S(2)}, u32[]{:S(2)}) collective-permute-start(bf16[160,512]{1,0:T(8,128)(2,1)S(1)} %get-tuple-element.61), channel_id=1, source_target_pairs={{0,8},{1,25},{2,10},{3,27},{4,12},{5,29},{6,14},{7,31},{8,16},{9,1... | collective-permute-start | bytes 491528 | tf_op jit(solution)/shard_map/ppermute | solution.py:29
  36.4 1.6 %copy-done = bf16[1,128,8192]{2,1,0:T(8,128)(2,1)S(1)} copy-done((bf16[1,128,8192]{2,1,0:T(8,128)(2,1)S(1)}, bf16[1,128,8192]{2,1,0:T(8,128)(2,1)}, u32[]{:S(2)}) %copy-start) | copy-done | bytes 2097176
  38.0 1.2 pick.1
  39.3 1.2 collective-permute-done.4
  40.4 4.4 %collective-permute-start.6 = (bf16[480,512]{1,0:T(8,128)(2,1)S(1)}, bf16[480,512]{1,0:T(8,128)(2,1)S(1)}, u32[]{:S(2)}, u32[]{:S(2)}) collective-permute-start(bf16[480,512]{1,0:T(8,128)(2,1)S(1)} %constant_dynamic-update-slice_fusion), channel_id=1, source_target_pairs={{0,6},{1,7},{2,0},{3,1},{4,2},{5,3},{6,4},{7,5},{8,14},{9,15},{10,... | collective-permute-start | bytes 1474568 | tf_op jit(solution)/shard_map/ppermute | solution.py:29
  44.8 1.9 %collective-permute-start.5 = (bf16[480,512]{1,0:T(8,128)(2,1)S(1)}, bf16[480,512]{1,0:T(8,128)(2,1)S(1)}, u32[]{:S(2)}, u32[]{:S(2)}) collective-permute-start(bf16[480,512]{1,0:T(8,128)(2,1)S(1)} %constant_dynamic-update-slice_fusion), channel_id=1, source_target_pairs={{0,2},{1,3},{2,4},{3,5},{4,6},{5,7},{6,0},{7,1},{8,10},{9,11},{10,... | collective-permute-start | bytes 1474568 | tf_op jit(solution)/shard_map/ppermute | solution.py:29
  46.8 7.5 %collective-permute-start.10 = (bf16[128,5120]{1,0:T(8,128)(2,1)S(1)}, bf16[128,5120]{1,0:T(8,128)(2,1)S(1)}, u32[]{:S(2)}, u32[]{:S(2)}) collective-permute-start(bf16[128,5120]{1,0:T(8,128)(2,1)S(1)} %get-tuple-element.43), channel_id=1, source_target_pairs={{0,32},{32,0},{64,96},{96,64},{128,160},{160,128},{192,224},{224,1... | collective-permute-start | bytes 3932168 | tf_op jit(solution)/shard_map/ppermute | solution.py:34
  54.4 1.2 collective-permute-done.5
  55.7 8.4 %collective-permute-start.8 = (bf16[960,512]{1,0:T(8,128)(2,1)S(1)}, bf16[960,512]{1,0:T(8,128)(2,1)S(1)}, u32[]{:S(2)}, u32[]{:S(2)}) collective-permute-start(bf16[960,512]{1,0:T(8,128)(2,1)S(1)} %constant_dynamic-update-slice_fusion.7.sides), channel_id=1, source_target_pairs={{0,1},{1,0},{2,3},{3,2},{4,5},{5,4},{6,7},{7,6},{8,9},{9,8},{10,11... | collective-permute-start | bytes 2949128 | tf_op jit(solution)/shard_map/ppermute | solution.py:29
  64.1 1.9 %collective-permute-start.7 = (bf16[960,512]{1,0:T(8,128)(2,1)S(1)}, bf16[960,512]{1,0:T(8,128)(2,1)S(1)}, u32[]{:S(2)}, u32[]{:S(2)}) collective-permute-start(bf16[960,512]{1,0:T(8,128)(2,1)S(1)} %constant_dynamic-update-slice_fusion.3.early), channel_id=1, source_target_pairs={{0,1},{1,0},{2,3},{3,2},{4,5},{5,4},{6,7},{7,6},{8,9},{9,8},{10,11... | collective-permute-start | bytes 2949128 | tf_op jit(solution)/shard_map/ppermute | solution.py:29
  66.2 1.9 %collective-permute-start.9 = (bf16[640,512]{1,0:T(8,128)(2,1)S(1)}, bf16[640,512]{1,0:T(8,128)(2,1)S(1)}, u32[]{:S(2)}, u32[]{:S(2)}) collective-permute-start(bf16[640,512]{1,0:T(8,128)(2,1)S(1)} %maximum_select_fusion), channel_id=1, source_target_pairs={{0,2},{1,7},{2,4},{3,1},{4,6},{5,3},{6,0},{7,5},{8,10},{9,15},{10,... | collective-permute-start | bytes 1966088 | tf_op jit(solution)/shard_map/ppermute | solution.py:29
  68.6 6.3 %stage.1 = (bf16[5120,512]{1,0:T(8,128)(2,1)S(1)}, bf16[256,5120]{1,0:T(8,128)(2,1)S(1)}, f32[8,128]{1,0:T(8,128)S(1)}) custom-call(s32[24]{0:T(128)S(1)} %concatenate.18.info, bf16[128,5120]{1,0:T(8,128)(2,1)S(1)} %get-tuple-element.33.own_rows, bf16[960,512]{1,0:T(8,128)(2,1)S(1)} %constant_dynamic-update-slice_fusion.3.early, ...), custom_call_target="tpu_custom_call" | custom-call | tf_op jit(solution)/shard_map/stage/pallas_call | solution.py:113
  74.9 3.0 %collective-permute-done.9.late = bf16[640,512]{1,0:T(8,128)(2,1)S(1)} collective-permute-done((bf16[640,512]{1,0:T(8,128)(2,1)S(1)}, bf16[640,512]{1,0:T(8,128)(2,1)S(1)}, u32[]{:S(2)}, u32[]{:S(2)}) %collective-permute-start.9) | collective-permute-done | bytes 655392 | tf_op jit(solution)/shard_map/ppermute | solution.py:29
  77.9 3.0 %collective-permute-done.10.rows = bf16[128,5120]{1,0:T(8,128)(2,1)S(1)} collective-permute-done((bf16[128,5120]{1,0:T(8,128)(2,1)S(1)}, bf16[128,5120]{1,0:T(8,128)(2,1)S(1)}, u32[]{:S(2)}, u32[]{:S(2)}) %collective-permute-start.10) | collective-permute-done | bytes 1310752 | tf_op jit(solution)/shard_map/ppermute | solution.py:34
  80.8 5.2 %collective-permute-start.11 = (bf16[640,512]{1,0:T(8,128)(2,1)S(1)}, bf16[640,512]{1,0:T(8,128)(2,1)S(1)}, u32[]{:S(2)}, u32[]{:S(2)}) collective-permute-start(bf16[640,512]{1,0:T(8,128)(2,1)S(1)} %collective-permute-done.9.late), channel_id=1, source_target_pairs={{0,1},{1,0},{2,3},{3,2},{4,5},{5,4},{6,7},{7,6},{8,9},{9,8},{10,11... | collective-permute-start | bytes 1966088 | tf_op jit(solution)/shard_map/ppermute | solution.py:29
  86.0 1.7 %collective-permute-done.11.late_swapped = bf16[640,512]{1,0:T(8,128)(2,1)S(1)} collective-permute-done((bf16[640,512]{1,0:T(8,128)(2,1)S(1)}, bf16[640,512]{1,0:T(8,128)(2,1)S(1)}, u32[]{:S(2)}, u32[]{:S(2)}) %collective-permute-start.11) | collective-permute-done | bytes 655392 | tf_op jit(solution)/shard_map/ppermute | solution.py:29
  87.7 4.2 %product.1 = (bf16[5120,512]{1,0:T(8,128)(2,1)S(1)}, bf16[256,5120]{1,0:T(8,128)(2,1)S(1)}, f32[128,512]{1,0:T(8,128)S(1)}, f32[128,512]{1,0:T(8,128)S(1)}, bf16[512,256]{1,0:T(8,128)(2,1)S(1)}) custom-call(s32[24]{0:T(128)S(1)} %concatenate.18.info, bf16[5120,512]{1,0:T(8,128)(2,1)S(1)} %get-tuple-element.41._, ...), custom_call_target="tpu_custom_call", output_to_operand_aliasing={{0}: (1, {}), {1}: (2, {})} | custom-call | tf_op jit(solution)/shard_map/product/pallas_call | solution.py:165
  91.9 10.9 %all_to_all.22 = bf16[8,64,256]{2,1,0:T(8,128)(2,1)S(1)} all-to-all(bf16[8,64,256]{2,1,0:T(8,128)(2,1)S(1)} %bitcast.21), channel_id=1, replica_groups={{0,1,2,3,4,5,6,7},{8,9,10,11,12,13,14,15},{16,17,18,19,20,21,22,23},{24..., dimensions={0} | all-to-all | bytes 524288 | tf_op jit(solution)/shard_map/all_to_all | solution.py:317
  102.8 1.9 %partial.1 = f32[256,128]{1,0:T(8,128)} custom-call(s32[24]{0:T(128)S(1)} %concatenate.18.info, bf16[512,256]{1,0:T(8,128)(2,1)S(1)} %bitcast.20, bf16[5120,512]{1,0:T(8,128)(2,1)S(1)} %get-tuple-element.51.factor), custom_call_target="tpu_custom_call" | custom-call | tf_op jit(solution)/shard_map/partial/pallas_call | solution.py:206
  104.7 7.3 %all-to-all-start.1 = ((f32[32,8,128]{2,1,0:T(8,128)}), f32[32,8,128]{2,1,0:T(8,128)S(1)}, u32[]{:S(2)}, u32[]{:S(2)}) async-start(f32[32,8,128]{2,1,0:T(8,128)} %bitcast.13), calls=%async_computation.1 | async-start | bytes 262144 | tf_op jit(solution)/shard_map/all_to_all | solution.py:320
  112.0 4.4 %collective-permute-start.12 = (f32[128,512]{1,0:T(8,128)S(1)}, f32[128,512]{1,0:T(8,128)S(1)}, u32[]{:S(2)}, u32[]{:S(2)}) collective-permute-start(f32[128,512]{1,0:T(8,128)S(1)} %get-tuple-element.49), channel_id=1, source_target_pairs={{0,32},{32,0},{64,96},{96,64},{128,160},{160,128},{192,224},{224,1... | collective-permute-start | bytes 786440 | tf_op jit(solution)/shard_map/ppermute | solution.py:34
  116.5 10.4 %collective-permute-done.12 = f32[128,512]{1,0:T(8,128)S(1)} collective-permute-done((f32[128,512]{1,0:T(8,128)S(1)}, f32[128,512]{1,0:T(8,128)S(1)}, u32[]{:S(2)}, u32[]{:S(2)}) %collective-permute-start.12) | collective-permute-done | bytes 262176 | tf_op jit(solution)/shard_map/ppermute | solution.py:34
  126.9 1.2 copy.13
  128.2 0.7 copy-done.1
  128.9 1.6 %total.1 = f32[16,512]{1,0:T(8,128)} custom-call(f32[256,128]{1,0:T(8,128)} %bitcast.23, f32[16,512]{1,0:T(8,128)} %bitcast.30), custom_call_target="tpu_custom_call" | custom-call | tf_op jit(solution)/shard_map/total/pallas_call | solution.py:241
  (35 shorter events, 1.7 us)
Async XLA Ops:
  0.6 27.5 %collective-permute-start.3 = (bf16[160,512]{1,0:T(8,128)(2,1)}, bf16[160,512]{1,0:T(8,128)(2,1)S(1)}, u32[]{:S(2)}, u32[]{:S(2)}) collective-permute-start(bf16[160,512]{1,0:T(8,128)(2,1)} %bitcast.25), channel_id=1, source_target_pairs={{0,24},{1,25},{2,26},{3,27},{4,28},{5,29},{6,30},{7,31},{8,0},{9,1... | collective-permute-start | bytes 491528 | tf_op jit(solution)/shard_map/ppermute | solution.py:29
  13.9 14.2 %collective-permute-start.2 = (bf16[160,512]{1,0:T(8,128)(2,1)}, bf16[160,512]{1,0:T(8,128)(2,1)S(1)}, u32[]{:S(2)}, u32[]{:S(2)}) collective-permute-start(bf16[160,512]{1,0:T(8,128)(2,1)} %bitcast.26), channel_id=1, source_target_pairs={{0,8},{1,9},{2,10},{3,11},{4,12},{5,13},{6,14},{7,15},{8,16},{9,17... | collective-permute-start | bytes 491528 | tf_op jit(solution)/shard_map/ppermute | solution.py:29
  15.9 12.3 %collective-permute-start.1 = (bf16[160,512]{1,0:T(8,128)(2,1)}, bf16[160,512]{1,0:T(8,128)(2,1)S(1)}, u32[]{:S(2)}, u32[]{:S(2)}) collective-permute-start(bf16[160,512]{1,0:T(8,128)(2,1)} %bitcast.27), channel_id=1, source_target_pairs={{0,6},{1,7},{2,0},{3,1},{4,2},{5,3},{6,4},{7,5},{8,14},{9,15},{10,... | collective-permute-start | bytes 491528 | tf_op jit(solution)/shard_map/ppermute | solution.py:29
  20.3 7.9 %collective-permute-start = (bf16[160,512]{1,0:T(8,128)(2,1)}, bf16[160,512]{1,0:T(8,128)(2,1)S(1)}, u32[]{:S(2)}, u32[]{:S(2)}) collective-permute-start(bf16[160,512]{1,0:T(8,128)(2,1)} %bitcast.28), channel_id=1, source_target_pairs={{0,2},{1,3},{2,4},{3,5},{4,6},{5,7},{6,0},{7,1},{8,10},{9,11},{10,... | collective-permute-start | bytes 491528 | tf_op jit(solution)/shard_map/ppermute | solution.py:29
  28.2 18.6 %copy-start.2 = (bf16[1,160,512]{2,1,0:T(8,128)(2,1)S(1)}, bf16[1,160,512]{2,1,0:T(8,128)(2,1)}, u32[]{:S(2)}) copy-start(bf16[1,160,512]{2,1,0:T(8,128)(2,1)} %param.5) | copy-start | bytes 491524
  28.2 12.2 %collective-permute-start.4 = (bf16[160,512]{1,0:T(8,128)(2,1)S(1)}, bf16[160,512]{1,0:T(8,128)(2,1)S(1)}, u32[]{:S(2)}, u32[]{:S(2)}) collective-permute-start(bf16[160,512]{1,0:T(8,128)(2,1)S(1)} %get-tuple-element.61), channel_id=1, source_target_pairs={{0,8},{1,25},{2,10},{3,27},{4,12},{5,29},{6,14},{7,31},{8,16},{9,1... | collective-permute-start | bytes 491528 | tf_op jit(solution)/shard_map/ppermute | solution.py:29
  36.4 1.6 %copy-start = (bf16[1,128,8192]{2,1,0:T(8,128)(2,1)S(1)}, bf16[1,128,8192]{2,1,0:T(8,128)(2,1)}, u32[]{:S(2)}) copy-start(bf16[1,128,8192]{2,1,0:T(8,128)(2,1)} %param.4) | copy-start | bytes 6291460
  40.4 13.9 %collective-permute-start.6 = (bf16[480,512]{1,0:T(8,128)(2,1)S(1)}, bf16[480,512]{1,0:T(8,128)(2,1)S(1)}, u32[]{:S(2)}, u32[]{:S(2)}) collective-permute-start(bf16[480,512]{1,0:T(8,128)(2,1)S(1)} %constant_dynamic-update-slice_fusion), channel_id=1, source_target_pairs={{0,6},{1,7},{2,0},{3,1},{4,2},{5,3},{6,4},{7,5},{8,14},{9,15},{10,... | collective-permute-start | bytes 1474568 | tf_op jit(solution)/shard_map/ppermute | solution.py:29
  44.8 10.8 %collective-permute-start.5 = (bf16[480,512]{1,0:T(8,128)(2,1)S(1)}, bf16[480,512]{1,0:T(8,128)(2,1)S(1)}, u32[]{:S(2)}, u32[]{:S(2)}) collective-permute-start(bf16[480,512]{1,0:T(8,128)(2,1)S(1)} %constant_dynamic-update-slice_fusion), channel_id=1, source_target_pairs={{0,2},{1,3},{2,4},{3,5},{4,6},{5,7},{6,0},{7,1},{8,10},{9,11},{10,... | collective-permute-start | bytes 1474568 | tf_op jit(solution)/shard_map/ppermute | solution.py:29
  46.8 34.0 %collective-permute-start.10 = (bf16[128,5120]{1,0:T(8,128)(2,1)S(1)}, bf16[128,5120]{1,0:T(8,128)(2,1)S(1)}, u32[]{:S(2)}, u32[]{:S(2)}) collective-permute-start(bf16[128,5120]{1,0:T(8,128)(2,1)S(1)} %get-tuple-element.43), channel_id=1, source_target_pairs={{0,32},{32,0},{64,96},{96,64},{128,160},{160,128},{192,224},{224,1... | collective-permute-start | bytes 3932168 | tf_op jit(solution)/shard_map/ppermute | solution.py:34
  55.7 12.5 %collective-permute-start.8 = (bf16[960,512]{1,0:T(8,128)(2,1)S(1)}, bf16[960,512]{1,0:T(8,128)(2,1)S(1)}, u32[]{:S(2)}, u32[]{:S(2)}) collective-permute-start(bf16[960,512]{1,0:T(8,128)(2,1)S(1)} %constant_dynamic-update-slice_fusion.7.sides), channel_id=1, source_target_pairs={{0,1},{1,0},{2,3},{3,2},{4,5},{5,4},{6,7},{7,6},{8,9},{9,8},{10,11... | collective-permute-start | bytes 2949128 | tf_op jit(solution)/shard_map/ppermute | solution.py:29
  64.1 4.5 %collective-permute-start.7 = (bf16[960,512]{1,0:T(8,128)(2,1)S(1)}, bf16[960,512]{1,0:T(8,128)(2,1)S(1)}, u32[]{:S(2)}, u32[]{:S(2)}) collective-permute-start(bf16[960,512]{1,0:T(8,128)(2,1)S(1)} %constant_dynamic-update-slice_fusion.3.early), channel_id=1, source_target_pairs={{0,1},{1,0},{2,3},{3,2},{4,5},{5,4},{6,7},{7,6},{8,9},{9,8},{10,11... | collective-permute-start | bytes 2949128 | tf_op jit(solution)/shard_map/ppermute | solution.py:29
  66.2 11.6 %collective-permute-start.9 = (bf16[640,512]{1,0:T(8,128)(2,1)S(1)}, bf16[640,512]{1,0:T(8,128)(2,1)S(1)}, u32[]{:S(2)}, u32[]{:S(2)}) collective-permute-start(bf16[640,512]{1,0:T(8,128)(2,1)S(1)} %maximum_select_fusion), channel_id=1, source_target_pairs={{0,2},{1,7},{2,4},{3,1},{4,6},{5,3},{6,0},{7,5},{8,10},{9,15},{10,... | collective-permute-start | bytes 1966088 | tf_op jit(solution)/shard_map/ppermute | solution.py:29
  80.8 6.9 %collective-permute-start.11 = (bf16[640,512]{1,0:T(8,128)(2,1)S(1)}, bf16[640,512]{1,0:T(8,128)(2,1)S(1)}, u32[]{:S(2)}, u32[]{:S(2)}) collective-permute-start(bf16[640,512]{1,0:T(8,128)(2,1)S(1)} %collective-permute-done.9.late), channel_id=1, source_target_pairs={{0,1},{1,0},{2,3},{3,2},{4,5},{5,4},{6,7},{7,6},{8,9},{9,8},{10,11... | collective-permute-start | bytes 1966088 | tf_op jit(solution)/shard_map/ppermute | solution.py:29
  104.7 23.5 %all-to-all-start.1 = ((f32[32,8,128]{2,1,0:T(8,128)}), f32[32,8,128]{2,1,0:T(8,128)S(1)}, u32[]{:S(2)}, u32[]{:S(2)}) async-start(f32[32,8,128]{2,1,0:T(8,128)} %bitcast.13), calls=%async_computation.1 | async-start | bytes 262144 | tf_op jit(solution)/shard_map/all_to_all | solution.py:320
  112.0 14.8 %collective-permute-start.12 = (f32[128,512]{1,0:T(8,128)S(1)}, f32[128,512]{1,0:T(8,128)S(1)}, u32[]{:S(2)}, u32[]{:S(2)}) collective-permute-start(f32[128,512]{1,0:T(8,128)S(1)} %get-tuple-element.49), channel_id=1, source_target_pairs={{0,32},{32,0},{64,96},{96,64},{128,160},{160,128},{192,224},{224,1... | collective-permute-start | bytes 786440 | tf_op jit(solution)/shard_map/ppermute | solution.py:34
  128.2 0.7 copy-start.1

commit v4 on v3

--- a/solution.py
+++ b/solution.py
@@ -237,7 +237,7 @@
 
 
 def total(terms, diagonal):
-    hbm = pl.BlockSpec(memory_space=pl.ANY)
+    hbm = pl.BlockSpec(memory_space=pltpu.MemorySpace.HBM)
     return pl.pallas_call(
         total_kernel,
         out_shape=jax.ShapeDtypeStruct((NC // NBLK, NC), jnp.float32),

time: 133 us -> 133 us (level)
  no operation moved by 1% of the time
where the time goes in v4:
time: 133 us; the launch traced here: 130 us
  starting transfers between devices  72.7 us (55%)
  waiting for transfers between devices  24.6 us (18%)
  Pallas kernels  15.2 us (11%)
  blocking collectives  10.9 us (8%)
  local copies, waits for them, and re-layouts  4.59 us (3%)
  other arithmetic  1.44 us (1%)
    ppermute x11, starting transfers between devices, ring(): return lax.ppermute(value, 'blk', pairs)  53.4 us
    ppermute x2, waiting for transfers between devices, partner(): return lax.ppermute(value, 'front', pairs)  13.3 us
    ppermute x2, starting transfers between devices, partner(): return lax.ppermute(value, 'front', pairs)  12 us
    ppermute x11, waiting for transfers between devices, ring(): return lax.ppermute(value, 'blk', pairs)  11.2 us
    all_to_all x1, blocking collectives, body(): lax.all_to_all(turned, 'blk', 0, 0, axis_index_groups=groups, tiled=True)  10.9 us
    all_to_all x1, starting transfers between devices, body(): lax.all_to_all(partial(info, turned, factor), 'blk', 0, 0, tiled=True)  7.33 us
    pallas_call x1, Pallas kernels, stage(): pl.pallas_call(stage_kernel, out_shape=[pltpu.VMEM((SROWS, NC), jnp.bfloa...  6.31 us
    pallas_call x1, Pallas kernels, product(): pl.pallas_call(product_kernel, out_shape=[pltpu.VMEM((SROWS, NC), jnp.bfl...  4.22 us
  transfers between devices with their start and end apart: 14, of which 9 were waited for; matrix products, arithmetic and copies ran while one was open for 3% of the time, Pallas kernels for 6%

profile of v4, /device:TPU:1, one launch (start us, length us, event | category | flops | bytes accessed | tf_op | source)
XLA Modules:
  0.0 130.4 jit_solution(18248573756070672848)
XLA Ops:
  0.6 13.3 %collective-permute-start.3 = (bf16[160,512]{1,0:T(8,128)(2,1)}, bf16[160,512]{1,0:T(8,128)(2,1)S(1)}, u32[]{:S(2)}, u32[]{:S(2)}) collective-permute-start(bf16[160,512]{1,0:T(8,128)(2,1)} %bitcast.25), channel_id=1, source_target_pairs={{0,24},{1,25},{2,26},{3,27},{4,28},{5,29},{6,30},{7,31},{8,0},{9,1... | collective-permute-start | bytes 491528 | tf_op jit(solution)/shard_map/ppermute | solution.py:29
  13.9 1.9 %collective-permute-start.2 = (bf16[160,512]{1,0:T(8,128)(2,1)}, bf16[160,512]{1,0:T(8,128)(2,1)S(1)}, u32[]{:S(2)}, u32[]{:S(2)}) collective-permute-start(bf16[160,512]{1,0:T(8,128)(2,1)} %bitcast.26), channel_id=1, source_target_pairs={{0,8},{1,9},{2,10},{3,11},{4,12},{5,13},{6,14},{7,15},{8,16},{9,17... | collective-permute-start | bytes 491528 | tf_op jit(solution)/shard_map/ppermute | solution.py:29
  15.9 4.4 %collective-permute-start.1 = (bf16[160,512]{1,0:T(8,128)(2,1)}, bf16[160,512]{1,0:T(8,128)(2,1)S(1)}, u32[]{:S(2)}, u32[]{:S(2)}) collective-permute-start(bf16[160,512]{1,0:T(8,128)(2,1)} %bitcast.27), channel_id=1, source_target_pairs={{0,6},{1,7},{2,0},{3,1},{4,2},{5,3},{6,4},{7,5},{8,14},{9,15},{10,... | collective-permute-start | bytes 491528 | tf_op jit(solution)/shard_map/ppermute | solution.py:29
  20.3 1.9 %collective-permute-start = (bf16[160,512]{1,0:T(8,128)(2,1)}, bf16[160,512]{1,0:T(8,128)(2,1)S(1)}, u32[]{:S(2)}, u32[]{:S(2)}) collective-permute-start(bf16[160,512]{1,0:T(8,128)(2,1)} %bitcast.28), channel_id=1, source_target_pairs={{0,2},{1,3},{2,4},{3,5},{4,6},{5,7},{6,0},{7,1},{8,10},{9,11},{10,... | collective-permute-start | bytes 491528 | tf_op jit(solution)/shard_map/ppermute | solution.py:29
  22.3 0.7 constant_dynamic-slice_fusion
  23.0 0.7 broadcast_select_fusion.1.lists
  24.5 3.7 %collective-permute-done.3 = bf16[160,512]{1,0:T(8,128)(2,1)S(1)} collective-permute-done((bf16[160,512]{1,0:T(8,128)(2,1)}, bf16[160,512]{1,0:T(8,128)(2,1)S(1)}, u32[]{:S(2)}, u32[]{:S(2)}) %collective-permute-start.3) | collective-permute-done | bytes 163872 | tf_op jit(solution)/shard_map/ppermute | solution.py:29
  28.2 8.2 %collective-permute-start.4 = (bf16[160,512]{1,0:T(8,128)(2,1)S(1)}, bf16[160,512]{1,0:T(8,128)(2,1)S(1)}, u32[]{:S(2)}, u32[]{:S(2)}) collective-permute-start(bf16[160,512]{1,0:T(8,128)(2,1)S(1)} %get-tuple-element.61), channel_id=1, source_target_pairs={{0,8},{1,25},{2,10},{3,27},{4,12},{5,29},{6,14},{7,31},{8,16},{9,1... | collective-permute-start | bytes 491528 | tf_op jit(solution)/shard_map/ppermute | solution.py:29
  36.4 1.6 %copy-done = bf16[1,128,8192]{2,1,0:T(8,128)(2,1)S(1)} copy-done((bf16[1,128,8192]{2,1,0:T(8,128)(2,1)S(1)}, bf16[1,128,8192]{2,1,0:T(8,128)(2,1)}, u32[]{:S(2)}) %copy-start) | copy-done | bytes 2097176
  38.0 1.2 pick.1
  39.3 1.1 collective-permute-done.4
  40.4 4.4 %collective-permute-start.6 = (bf16[480,512]{1,0:T(8,128)(2,1)S(1)}, bf16[480,512]{1,0:T(8,128)(2,1)S(1)}, u32[]{:S(2)}, u32[]{:S(2)}) collective-permute-start(bf16[480,512]{1,0:T(8,128)(2,1)S(1)} %constant_dynamic-update-slice_fusion), channel_id=1, source_target_pairs={{0,6},{1,7},{2,0},{3,1},{4,2},{5,3},{6,4},{7,5},{8,14},{9,15},{10,... | collective-permute-start | bytes 1474568 | tf_op jit(solution)/shard_map/ppermute | solution.py:29
  44.8 1.9 %collective-permute-start.5 = (bf16[480,512]{1,0:T(8,128)(2,1)S(1)}, bf16[480,512]{1,0:T(8,128)(2,1)S(1)}, u32[]{:S(2)}, u32[]{:S(2)}) collective-permute-start(bf16[480,512]{1,0:T(8,128)(2,1)S(1)} %constant_dynamic-update-slice_fusion), channel_id=1, source_target_pairs={{0,2},{1,3},{2,4},{3,5},{4,6},{5,7},{6,0},{7,1},{8,10},{9,11},{10,... | collective-permute-start | bytes 1474568 | tf_op jit(solution)/shard_map/ppermute | solution.py:29
  46.8 7.5 %collective-permute-start.10 = (bf16[128,5120]{1,0:T(8,128)(2,1)S(1)}, bf16[128,5120]{1,0:T(8,128)(2,1)S(1)}, u32[]{:S(2)}, u32[]{:S(2)}) collective-permute-start(bf16[128,5120]{1,0:T(8,128)(2,1)S(1)} %get-tuple-element.43), channel_id=1, source_target_pairs={{0,32},{32,0},{64,96},{96,64},{128,160},{160,128},{192,224},{224,1... | collective-permute-start | bytes 3932168 | tf_op jit(solution)/shard_map/ppermute | solution.py:34
  54.4 1.2 collective-permute-done.5
  55.7 8.4 %collective-permute-start.8 = (bf16[960,512]{1,0:T(8,128)(2,1)S(1)}, bf16[960,512]{1,0:T(8,128)(2,1)S(1)}, u32[]{:S(2)}, u32[]{:S(2)}) collective-permute-start(bf16[960,512]{1,0:T(8,128)(2,1)S(1)} %constant_dynamic-update-slice_fusion.7.sides), channel_id=1, source_target_pairs={{0,1},{1,0},{2,3},{3,2},{4,5},{5,4},{6,7},{7,6},{8,9},{9,8},{10,11... | collective-permute-start | bytes 2949128 | tf_op jit(solution)/shard_map/ppermute | solution.py:29
  64.1 1.9 %collective-permute-start.7 = (bf16[960,512]{1,0:T(8,128)(2,1)S(1)}, bf16[960,512]{1,0:T(8,128)(2,1)S(1)}, u32[]{:S(2)}, u32[]{:S(2)}) collective-permute-start(bf16[960,512]{1,0:T(8,128)(2,1)S(1)} %constant_dynamic-update-slice_fusion.3.early), channel_id=1, source_target_pairs={{0,1},{1,0},{2,3},{3,2},{4,5},{5,4},{6,7},{7,6},{8,9},{9,8},{10,11... | collective-permute-start | bytes 2949128 | tf_op jit(solution)/shard_map/ppermute | solution.py:29
  66.2 1.9 %collective-permute-start.9 = (bf16[640,512]{1,0:T(8,128)(2,1)S(1)}, bf16[640,512]{1,0:T(8,128)(2,1)S(1)}, u32[]{:S(2)}, u32[]{:S(2)}) collective-permute-start(bf16[640,512]{1,0:T(8,128)(2,1)S(1)} %maximum_select_fusion), channel_id=1, source_target_pairs={{0,2},{1,7},{2,4},{3,1},{4,6},{5,3},{6,0},{7,5},{8,10},{9,15},{10,... | collective-permute-start | bytes 1966088 | tf_op jit(solution)/shard_map/ppermute | solution.py:29
  68.6 6.3 %stage.1 = (bf16[5120,512]{1,0:T(8,128)(2,1)S(1)}, bf16[256,5120]{1,0:T(8,128)(2,1)S(1)}, f32[8,128]{1,0:T(8,128)S(1)}) custom-call(s32[24]{0:T(128)S(1)} %concatenate.18.info, bf16[128,5120]{1,0:T(8,128)(2,1)S(1)} %get-tuple-element.33.own_rows, bf16[960,512]{1,0:T(8,128)(2,1)S(1)} %constant_dynamic-update-slice_fusion.3.early, ...), custom_call_target="tpu_custom_call" | custom-call | tf_op jit(solution)/shard_map/stage/pallas_call | solution.py:113
  74.9 3.0 %collective-permute-done.9.late = bf16[640,512]{1,0:T(8,128)(2,1)S(1)} collective-permute-done((bf16[640,512]{1,0:T(8,128)(2,1)S(1)}, bf16[640,512]{1,0:T(8,128)(2,1)S(1)}, u32[]{:S(2)}, u32[]{:S(2)}) %collective-permute-start.9) | collective-permute-done | bytes 655392 | tf_op jit(solution)/shard_map/ppermute | solution.py:29
  77.9 3.0 %collective-permute-done.10.rows = bf16[128,5120]{1,0:T(8,128)(2,1)S(1)} collective-permute-done((bf16[128,5120]{1,0:T(8,128)(2,1)S(1)}, bf16[128,5120]{1,0:T(8,128)(2,1)S(1)}, u32[]{:S(2)}, u32[]{:S(2)}) %collective-permute-start.10) | collective-permute-done | bytes 1310752 | tf_op jit(solution)/shard_map/ppermute | solution.py:34
  80.8 5.2 %collective-permute-start.11 = (bf16[640,512]{1,0:T(8,128)(2,1)S(1)}, bf16[640,512]{1,0:T(8,128)(2,1)S(1)}, u32[]{:S(2)}, u32[]{:S(2)}) collective-permute-start(bf16[640,512]{1,0:T(8,128)(2,1)S(1)} %collective-permute-done.9.late), channel_id=1, source_target_pairs={{0,1},{1,0},{2,3},{3,2},{4,5},{5,4},{6,7},{7,6},{8,9},{9,8},{10,11... | collective-permute-start | bytes 1966088 | tf_op jit(solution)/shard_map/ppermute | solution.py:29
  86.0 1.7 %collective-permute-done.11.late_swapped = bf16[640,512]{1,0:T(8,128)(2,1)S(1)} collective-permute-done((bf16[640,512]{1,0:T(8,128)(2,1)S(1)}, bf16[640,512]{1,0:T(8,128)(2,1)S(1)}, u32[]{:S(2)}, u32[]{:S(2)}) %collective-permute-start.11) | collective-permute-done | bytes 655392 | tf_op jit(solution)/shard_map/ppermute | solution.py:29
  87.7 4.2 %product.1 = (bf16[5120,512]{1,0:T(8,128)(2,1)S(1)}, bf16[256,5120]{1,0:T(8,128)(2,1)S(1)}, f32[128,512]{1,0:T(8,128)S(1)}, f32[128,512]{1,0:T(8,128)S(1)}, bf16[512,256]{1,0:T(8,128)(2,1)S(1)}) custom-call(s32[24]{0:T(128)S(1)} %concatenate.18.info, bf16[5120,512]{1,0:T(8,128)(2,1)S(1)} %get-tuple-element.41._, ...), custom_call_target="tpu_custom_call", output_to_operand_aliasing={{0}: (1, {}), {1}: (2, {})} | custom-call | tf_op jit(solution)/shard_map/product/pallas_call | solution.py:165
  91.9 10.9 %all_to_all.22 = bf16[8,64,256]{2,1,0:T(8,128)(2,1)S(1)} all-to-all(bf16[8,64,256]{2,1,0:T(8,128)(2,1)S(1)} %bitcast.21), channel_id=1, replica_groups={{0,1,2,3,4,5,6,7},{8,9,10,11,12,13,14,15},{16,17,18,19,20,21,22,23},{24..., dimensions={0} | all-to-all | bytes 524288 | tf_op jit(solution)/shard_map/all_to_all | solution.py:317
  102.8 1.9 %partial.1 = f32[256,128]{1,0:T(8,128)} custom-call(s32[24]{0:T(128)S(1)} %concatenate.18.info, bf16[512,256]{1,0:T(8,128)(2,1)S(1)} %bitcast.20, bf16[5120,512]{1,0:T(8,128)(2,1)S(1)} %get-tuple-element.51.factor), custom_call_target="tpu_custom_call" | custom-call | tf_op jit(solution)/shard_map/partial/pallas_call | solution.py:206
  104.7 7.3 %all-to-all-start.1 = ((f32[32,8,128]{2,1,0:T(8,128)}), f32[32,8,128]{2,1,0:T(8,128)S(1)}, u32[]{:S(2)}, u32[]{:S(2)}) async-start(f32[32,8,128]{2,1,0:T(8,128)} %bitcast.13), calls=%async_computation.1 | async-start | bytes 262144 | tf_op jit(solution)/shard_map/all_to_all | solution.py:320
  112.0 4.4 %collective-permute-start.12 = (f32[128,512]{1,0:T(8,128)S(1)}, f32[128,512]{1,0:T(8,128)S(1)}, u32[]{:S(2)}, u32[]{:S(2)}) collective-permute-start(f32[128,512]{1,0:T(8,128)S(1)} %get-tuple-element.49), channel_id=1, source_target_pairs={{0,32},{32,0},{64,96},{96,64},{128,160},{160,128},{192,224},{224,1... | collective-permute-start | bytes 786440 | tf_op jit(solution)/shard_map/ppermute | solution.py:34
  116.5 10.4 %collective-permute-done.12 = f32[128,512]{1,0:T(8,128)S(1)} collective-permute-done((f32[128,512]{1,0:T(8,128)S(1)}, f32[128,512]{1,0:T(8,128)S(1)}, u32[]{:S(2)}, u32[]{:S(2)}) %collective-permute-start.12) | collective-permute-done | bytes 262176 | tf_op jit(solution)/shard_map/ppermute | solution.py:34
  126.9 1.2 copy.13
  128.2 0.7 copy-done.1
  128.9 1.6 %total.1 = f32[16,512]{1,0:T(8,128)} custom-call(f32[256,128]{1,0:T(8,128)} %bitcast.23, f32[16,512]{1,0:T(8,128)} %bitcast.30), custom_call_target="tpu_custom_call" | custom-call | tf_op jit(solution)/shard_map/total/pallas_call | solution.py:241
  (35 shorter events, 1.7 us)
Async XLA Ops:
  0.6 27.5 %collective-permute-start.3 = (bf16[160,512]{1,0:T(8,128)(2,1)}, bf16[160,512]{1,0:T(8,128)(2,1)S(1)}, u32[]{:S(2)}, u32[]{:S(2)}) collective-permute-start(bf16[160,512]{1,0:T(8,128)(2,1)} %bitcast.25), channel_id=1, source_target_pairs={{0,24},{1,25},{2,26},{3,27},{4,28},{5,29},{6,30},{7,31},{8,0},{9,1... | collective-permute-start | bytes 491528 | tf_op jit(solution)/shard_map/ppermute | solution.py:29
  13.9 14.2 %collective-permute-start.2 = (bf16[160,512]{1,0:T(8,128)(2,1)}, bf16[160,512]{1,0:T(8,128)(2,1)S(1)}, u32[]{:S(2)}, u32[]{:S(2)}) collective-permute-start(bf16[160,512]{1,0:T(8,128)(2,1)} %bitcast.26), channel_id=1, source_target_pairs={{0,8},{1,9},{2,10},{3,11},{4,12},{5,13},{6,14},{7,15},{8,16},{9,17... | collective-permute-start | bytes 491528 | tf_op jit(solution)/shard_map/ppermute | solution.py:29
  15.9 12.3 %collective-permute-start.1 = (bf16[160,512]{1,0:T(8,128)(2,1)}, bf16[160,512]{1,0:T(8,128)(2,1)S(1)}, u32[]{:S(2)}, u32[]{:S(2)}) collective-permute-start(bf16[160,512]{1,0:T(8,128)(2,1)} %bitcast.27), channel_id=1, source_target_pairs={{0,6},{1,7},{2,0},{3,1},{4,2},{5,3},{6,4},{7,5},{8,14},{9,15},{10,... | collective-permute-start | bytes 491528 | tf_op jit(solution)/shard_map/ppermute | solution.py:29
  20.3 7.9 %collective-permute-start = (bf16[160,512]{1,0:T(8,128)(2,1)}, bf16[160,512]{1,0:T(8,128)(2,1)S(1)}, u32[]{:S(2)}, u32[]{:S(2)}) collective-permute-start(bf16[160,512]{1,0:T(8,128)(2,1)} %bitcast.28), channel_id=1, source_target_pairs={{0,2},{1,3},{2,4},{3,5},{4,6},{5,7},{6,0},{7,1},{8,10},{9,11},{10,... | collective-permute-start | bytes 491528 | tf_op jit(solution)/shard_map/ppermute | solution.py:29
  28.2 18.6 %copy-start.2 = (bf16[1,160,512]{2,1,0:T(8,128)(2,1)S(1)}, bf16[1,160,512]{2,1,0:T(8,128)(2,1)}, u32[]{:S(2)}) copy-start(bf16[1,160,512]{2,1,0:T(8,128)(2,1)} %param.5) | copy-start | bytes 491524
  28.2 12.2 %collective-permute-start.4 = (bf16[160,512]{1,0:T(8,128)(2,1)S(1)}, bf16[160,512]{1,0:T(8,128)(2,1)S(1)}, u32[]{:S(2)}, u32[]{:S(2)}) collective-permute-start(bf16[160,512]{1,0:T(8,128)(2,1)S(1)} %get-tuple-element.61), channel_id=1, source_target_pairs={{0,8},{1,25},{2,10},{3,27},{4,12},{5,29},{6,14},{7,31},{8,16},{9,1... | collective-permute-start | bytes 491528 | tf_op jit(solution)/shard_map/ppermute | solution.py:29
  36.4 1.6 %copy-start = (bf16[1,128,8192]{2,1,0:T(8,128)(2,1)S(1)}, bf16[1,128,8192]{2,1,0:T(8,128)(2,1)}, u32[]{:S(2)}) copy-start(bf16[1,128,8192]{2,1,0:T(8,128)(2,1)} %param.4) | copy-start | bytes 6291460
  40.4 13.9 %collective-permute-start.6 = (bf16[480,512]{1,0:T(8,128)(2,1)S(1)}, bf16[480,512]{1,0:T(8,128)(2,1)S(1)}, u32[]{:S(2)}, u32[]{:S(2)}) collective-permute-start(bf16[480,512]{1,0:T(8,128)(2,1)S(1)} %constant_dynamic-update-slice_fusion), channel_id=1, source_target_pairs={{0,6},{1,7},{2,0},{3,1},{4,2},{5,3},{6,4},{7,5},{8,14},{9,15},{10,... | collective-permute-start | bytes 1474568 | tf_op jit(solution)/shard_map/ppermute | solution.py:29
  44.8 10.8 %collective-permute-start.5 = (bf16[480,512]{1,0:T(8,128)(2,1)S(1)}, bf16[480,512]{1,0:T(8,128)(2,1)S(1)}, u32[]{:S(2)}, u32[]{:S(2)}) collective-permute-start(bf16[480,512]{1,0:T(8,128)(2,1)S(1)} %constant_dynamic-update-slice_fusion), channel_id=1, source_target_pairs={{0,2},{1,3},{2,4},{3,5},{4,6},{5,7},{6,0},{7,1},{8,10},{9,11},{10,... | collective-permute-start | bytes 1474568 | tf_op jit(solution)/shard_map/ppermute | solution.py:29
  46.8 34.0 %collective-permute-start.10 = (bf16[128,5120]{1,0:T(8,128)(2,1)S(1)}, bf16[128,5120]{1,0:T(8,128)(2,1)S(1)}, u32[]{:S(2)}, u32[]{:S(2)}) collective-permute-start(bf16[128,5120]{1,0:T(8,128)(2,1)S(1)} %get-tuple-element.43), channel_id=1, source_target_pairs={{0,32},{32,0},{64,96},{96,64},{128,160},{160,128},{192,224},{224,1... | collective-permute-start | bytes 3932168 | tf_op jit(solution)/shard_map/ppermute | solution.py:34
  55.7 12.5 %collective-permute-start.8 = (bf16[960,512]{1,0:T(8,128)(2,1)S(1)}, bf16[960,512]{1,0:T(8,128)(2,1)S(1)}, u32[]{:S(2)}, u32[]{:S(2)}) collective-permute-start(bf16[960,512]{1,0:T(8,128)(2,1)S(1)} %constant_dynamic-update-slice_fusion.7.sides), channel_id=1, source_target_pairs={{0,1},{1,0},{2,3},{3,2},{4,5},{5,4},{6,7},{7,6},{8,9},{9,8},{10,11... | collective-permute-start | bytes 2949128 | tf_op jit(solution)/shard_map/ppermute | solution.py:29
  64.1 4.5 %collective-permute-start.7 = (bf16[960,512]{1,0:T(8,128)(2,1)S(1)}, bf16[960,512]{1,0:T(8,128)(2,1)S(1)}, u32[]{:S(2)}, u32[]{:S(2)}) collective-permute-start(bf16[960,512]{1,0:T(8,128)(2,1)S(1)} %constant_dynamic-update-slice_fusion.3.early), channel_id=1, source_target_pairs={{0,1},{1,0},{2,3},{3,2},{4,5},{5,4},{6,7},{7,6},{8,9},{9,8},{10,11... | collective-permute-start | bytes 2949128 | tf_op jit(solution)/shard_map/ppermute | solution.py:29
  66.2 11.6 %collective-permute-start.9 = (bf16[640,512]{1,0:T(8,128)(2,1)S(1)}, bf16[640,512]{1,0:T(8,128)(2,1)S(1)}, u32[]{:S(2)}, u32[]{:S(2)}) collective-permute-start(bf16[640,512]{1,0:T(8,128)(2,1)S(1)} %maximum_select_fusion), channel_id=1, source_target_pairs={{0,2},{1,7},{2,4},{3,1},{4,6},{5,3},{6,0},{7,5},{8,10},{9,15},{10,... | collective-permute-start | bytes 1966088 | tf_op jit(solution)/shard_map/ppermute | solution.py:29
  80.8 6.9 %collective-permute-start.11 = (bf16[640,512]{1,0:T(8,128)(2,1)S(1)}, bf16[640,512]{1,0:T(8,128)(2,1)S(1)}, u32[]{:S(2)}, u32[]{:S(2)}) collective-permute-start(bf16[640,512]{1,0:T(8,128)(2,1)S(1)} %collective-permute-done.9.late), channel_id=1, source_target_pairs={{0,1},{1,0},{2,3},{3,2},{4,5},{5,4},{6,7},{7,6},{8,9},{9,8},{10,11... | collective-permute-start | bytes 1966088 | tf_op jit(solution)/shard_map/ppermute | solution.py:29
  104.7 23.5 %all-to-all-start.1 = ((f32[32,8,128]{2,1,0:T(8,128)}), f32[32,8,128]{2,1,0:T(8,128)S(1)}, u32[]{:S(2)}, u32[]{:S(2)}) async-start(f32[32,8,128]{2,1,0:T(8,128)} %bitcast.13), calls=%async_computation.1 | async-start | bytes 262144 | tf_op jit(solution)/shard_map/all_to_all | solution.py:320
  112.0 14.8 %collective-permute-start.12 = (f32[128,512]{1,0:T(8,128)S(1)}, f32[128,512]{1,0:T(8,128)S(1)}, u32[]{:S(2)}, u32[]{:S(2)}) collective-permute-start(f32[128,512]{1,0:T(8,128)S(1)} %get-tuple-element.49), channel_id=1, source_target_pairs={{0,32},{32,0},{64,96},{96,64},{128,160},{160,128},{192,224},{224,1... | collective-permute-start | bytes 786440 | tf_op jit(solution)/shard_map/ppermute | solution.py:34
  128.2 0.7 copy-start.1
